TPU v7x, 32 devices: a whole 2x2x4 slice. The times are simulated.
32 devices in a mesh: group: 2 (over x), lm: 8 (over z, y), env: 2 (over core).
Axes of the slice: x: 2, y: 2, z: 4, core: 2. Of those that a mesh axis runs over, the one named last changes fastest.
Arguments:
- env_desc: bfloat16 [1024, 512], P(('group', 'lm', 'env')), parts along dimension 0, may hold values from -6 to 6
- landmarks: bfloat16 [8192, 512], P(('lm', 'env')), may hold values from -6 to 6
- whitening: bfloat16 [8192, 1024], P(('lm', 'env')), may hold values from -120 to 120
Outputs:
- coords: float32 [1024, 1024], P(('group', 'lm', 'env')), parts along dimension 0
There are 2 independent parts, one for each index of `group`. A program takes and returns all parts, laid end to end along the dimension named above; an argument that names none is the same for every part. Nothing has to cross between parts.
All inputs are finite; a program needn't handle non-finite values.
Results may differ from a plain program's by a relative error of at most 0.0029.
Values may be sent and summed in bfloat16 or wider, within the bound.
No kernel may reach another device: no remote copies, remote signals or barrier semaphores. Data moves between devices by JAX's collectives and lax.ppermute only.
A program may use at most 64 MiB of HBM per device.

v0:
```python
import jax
import jax.numpy as jnp
from jax import lax
from jax.sharding import PartitionSpec as P


def kernel_block(rows, landmarks, land_sq, weights):
    row_sq = jnp.sum(jnp.square(rows.astype(jnp.float32)), axis=1)
    cross = lax.dot_general(
        rows, landmarks, (((1,), (1,)), ((), ())), preferred_element_type=jnp.float32
    )
    dist = row_sq[:, None] + land_sq[None, :] - 2.0 * cross
    kern = jnp.exp(-(4.0 / rows.shape[1]) * dist).astype(jnp.bfloat16)
    return jnp.dot(kern, weights, preferred_element_type=jnp.float32)


def local(env_desc, landmarks, whitening):
    land_sq = jnp.sum(jnp.square(landmarks.astype(jnp.float32)), axis=1)
    gathered = lax.all_gather(env_desc, ("lm", "env"), axis=0, tiled=True)
    return lax.psum_scatter(
        kernel_block(gathered, landmarks, land_sq, whitening),
        ("lm", "env"),
        scatter_dimension=0,
        tiled=True,
    )


def solution(mesh):
    return jax.shard_map(
        local,
        mesh=mesh,
        in_specs=(P(("group", "lm", "env"), None), P(("lm", "env"), None), P(("lm", "env"), None)),
        out_specs=P(("group", "lm", "env"), None),
        check_vma=False,
    )
```

profile of v0, /device:TPU:0, one launch (start us, length us, event | category | flops | bytes accessed | tf_op | source)
XLA Modules:
  0.0 102.2 jit_solution(5622019118653470272)
XLA Ops:
  6.5 0.0 copy-start
  6.5 0.0 reduce-scatter.2.cloned.1.call-start
  6.5 1.3 %multiply_reduce_fusion = f32[512]{0:T(512)S(1)} fusion(bf16[512,512]{1,0:T(8,128)(2,1)} %param.4), kind=kLoop, calls=%fused_computation.7 | loop fusion | flops 785920 | bytes 526336 | tf_op jit(solution)/shard_map/reduce_sum | solution.py:18
  7.8 24.8 %all_gather.3 = bf16[512,512]{1,0:T(8,128)(2,1)S(1)} all-gather(bf16[32,512]{1,0:T(8,128)(2,1)} %param.3), channel_id=1, replica_groups=mesh['group'=2,'lm'=8,'env'=2] {'lm','env'}, dimensions={0}, use_global_device_ids=true | all-gather | bytes 557056 | tf_op jit(solution)/shard_map/all_gather | solution.py:19
  32.6 0.2 multiply_reduce_fusion.1
  32.8 0.0 copy-done
  32.8 3.5 %fusion.4 = f32[512,1024]{1,0:T(8,128)} fusion(bf16[512,1024]{1,0:T(8,128)(2,1)S(1)} %copy-done, bf16[512,512]{1,0:T(8,128)(2,1)S(1)} %all_gather.3, bf16[512,512]{1,0:T(8,128)(2,1)} %param.4, f32[512]{0:T(512)S(1)} %multiply_reduce_fusion, f32[512]{0:T(512)S(1)} %multiply_reduce_fusion.1), kind=kOutput, calls=%fused_computation.5 | convolution fusion | flops 806617088 | bytes 4198400 | tf_op jit(solution)/shard_map/dot_general | solution.py:14
  36.3 0.0 reduce-scatter.2.cloned.1.call-update
  36.3 59.0 %reduce-scatter.2.cloned.1.call-done = f32[32,1024]{1,0:T(8,128)} async-done(((f32[512,1024]{1,0:T(8,128)}), f32[32,1024]{1,0:T(8,128)}) %reduce-scatter.2.cloned.1.call-update) | async-done | bytes 131088 | tf_op jit(solution)/shard_map/reduce_scatter | solution.py:20
Async XLA Ops:
  6.5 26.3 %copy-start = (bf16[512,1024]{1,0:T(8,128)(2,1)S(1)}, bf16[512,1024]{1,0:T(8,128)(2,1)}, u32[]{:S(2)}) copy-start(bf16[512,1024]{1,0:T(8,128)(2,1)} %param.5) | copy-start | bytes 3145732
  6.5 88.8 %reduce-scatter.2.cloned.1.call-start = ((), (), s32[]{:S(2)}) async-start(), calls=%async_computation.1 | async-start | bytes 2228224 | tf_op jit(solution)/shard_map/reduce_scatter | solution.py:20
Sparse Core Ops, SparseCore 0:
  36.5 58.8 reduce-scatter.1
where the time goes:
time: 102 us
  waiting for transfers between devices  59 us (58%)
  blocking collectives  24.8 us (24%)
  between operations  13.4 us (13%)
  matrix products  3.49 us (3%)
  other arithmetic  1.48 us (1%)
    reduce_scatter x1, waiting for transfers between devices, local(): lax.psum_scatter(kernel_block(gathered, landmarks, land_sq, whitening), (...  59 us
    all_gather x1, blocking collectives, local(): gathered = lax.all_gather(env_desc, ('lm', 'env'), axis=0, tiled=True)  24.8 us
    dot_general x1, matrix products, kernel_block(): return jnp.dot(kern, weights, preferred_element_type=jnp.float32)  3.49 us
  transfers between devices with their start and end apart: 1, of which 1 were waited for; matrix products, arithmetic and copies ran while one was open for 0% of the time, Pallas kernels for 0%

commit v1 on v0

v1 whole, which is shorter than its diff:
```python
import jax
import jax.numpy as jnp
from jax import lax
from jax.sharding import PartitionSpec as P

AXES = ("lm", "env")


def kernel_block(rows, landmarks, land_sq, weights):
    row_sq = jnp.sum(jnp.square(rows.astype(jnp.float32)), axis=1)
    cross = lax.dot_general(
        rows, landmarks, (((1,), (1,)), ((), ())), preferred_element_type=jnp.float32
    )
    dist = row_sq[:, None] + land_sq[None, :] - 2.0 * cross
    kern = jnp.exp(-(4.0 / rows.shape[1]) * dist).astype(jnp.bfloat16)
    return jnp.dot(kern, weights, preferred_element_type=jnp.float32)


def solution(mesh):
    chips = mesh.shape["lm"]
    inner = 1 << ((chips.bit_length() - 1) // 2)
    outer = chips // inner
    steps = ([0] + list(range(outer - 1, outer // 2, -1)), list(range(1, outer // 2 + 1)))

    swap = [(2 * chip + core, 2 * chip + 1 - core) for chip in range(chips) for core in range(2)]

    def exchange(block, by):
        pairs = [
            (2 * chip + core, 2 * (chip ^ by[core]) + core)
            for chip in range(chips)
            for core in range(2)
        ]
        return lax.ppermute(block, AXES, pairs)

    def local(env_desc, landmarks, whitening):
        rows = env_desc.shape[0]
        land_sq = jnp.sum(jnp.square(landmarks.astype(jnp.float32)), axis=1)

        chip_rows = jnp.concatenate([env_desc, lax.ppermute(env_desc, AXES, swap)])
        line = [chip_rows] + [exchange(chip_rows, (k, k)) for k in range(1, inner)]
        line = jnp.concatenate(line)
        got = [exchange(line, (a * inner, b * inner)) for a, b in reversed(list(zip(*steps)))]
        first = jnp.concatenate(got[::-1])
        second = lax.ppermute(first, AXES, swap)

        given = kernel_block(first, landmarks, land_sq, whitening).astype(jnp.bfloat16)
        taken = lax.ppermute(given, AXES, swap)
        sums = kernel_block(second, landmarks, land_sq, whitening)
        sums = (sums + taken.astype(jnp.float32)).astype(jnp.bfloat16)

        total = None
        blocks = sums.reshape(outer // 2, inner, 2 * rows, -1)
        for i in reversed(range(outer // 2)):
            for k in reversed(range(inner)):
                by = (steps[1][i] * inner + k, steps[0][i] * inner + k)
                part = exchange(blocks[i, k], by).astype(jnp.float32)
                total = part if total is None else total + part
        return total[rows:] + lax.ppermute(total[:rows], AXES, swap)

    return jax.shard_map(
        local,
        mesh=mesh,
        in_specs=(P(("group", "lm", "env"), None), P(("lm", "env"), None), P(("lm", "env"), None)),
        out_specs=P(("group", "lm", "env"), None),
        check_vma=False,
    )
```

time: 102 us -> 40.1 us (0.39)
  waiting for transfers between devices: 59 us -> 16.4 us
  blocking collectives: 24.8 us -> 0 us
  starting transfers between devices: 0.01 us -> 18.1 us
  between operations: 13.4 us -> 0.11 us
  matrix products: 3.49 us -> 2.23 us
    reduce_scatter x1 -> x0, waiting for transfers between devices: 59 us -> none  [local(): lax.psum_scatter(kernel_block(gathered, landmarks, land_sq, whitening), (...]
    all_gather x1 -> x0, blocking collectives: 24.8 us -> none  [local(): gathered = lax.all_gather(env_desc, ('lm', 'env'), axis=0, tiled=True)]
    ppermute x0 -> x11, starting transfers between devices: none -> 18.1 us  [the longest x7 15.4 us: exchange(): return lax.ppermute(block, AXES, pairs)]
    ppermute x0 -> x11, waiting for transfers between devices: none -> 16.4 us  [the longest x7 12.7 us: exchange(): return lax.ppermute(block, AXES, pairs)]
    dot_general x1 -> x2, matrix products: 3.49 us -> 2.23 us  [kernel_block(): return jnp.dot(kern, weights, preferred_element_type=jnp.float32)]
  transfers between devices with their start and end apart: 1 -> 11, of which waited for: 1 -> 8; matrix products, arithmetic and copies ran while one was open for 0% -> 5% of each run, Pallas kernels for 0% -> 0%
where the time goes in v1:
time: 40.1 us; the launch traced here: 39.9 us
  starting transfers between devices  18.1 us (45%)
  waiting for transfers between devices  16.4 us (41%)
  matrix products  2.23 us (6%)
  other arithmetic  2.22 us (6%)
  local copies, waits for them, and re-layouts  0.85 us (2%)
    ppermute x7, starting transfers between devices, exchange(): return lax.ppermute(block, AXES, pairs)  15.4 us
    ppermute x7, waiting for transfers between devices, exchange(): return lax.ppermute(block, AXES, pairs)  12.7 us
    dot_general x2, matrix products, kernel_block(): return jnp.dot(kern, weights, preferred_element_type=jnp.float32)  2.23 us
    ppermute x1, starting transfers between devices, local(): taken = lax.ppermute(given, AXES, swap)  2.15 us
    ppermute x1, waiting for transfers between devices, local(): second = lax.ppermute(first, AXES, swap)  1.77 us
    ppermute x1, waiting for transfers between devices, local(): return total[rows:] + lax.ppermute(total[:rows], AXES, swap)  1.33 us
    reduce_sum x1, other arithmetic, local(): land_sq = jnp.sum(jnp.square(landmarks.astype(jnp.float32)), axis=1)  1.22 us
  transfers between devices with their start and end apart: 11, of which 8 were waited for; matrix products, arithmetic and copies ran while one was open for 5% of the time, Pallas kernels for 0%

profile of v1, /device:TPU:0, one launch (start us, length us, event | category | flops | bytes accessed | tf_op | source)
XLA Modules:
  0.0 39.9 jit_solution(7620976868884690963)
XLA Ops:
  0.0 0.5 %collective-permute-start = (bf16[32,512]{1,0:T(8,128)(2,1)}, bf16[32,512]{1,0:T(8,128)(2,1)S(1)}, u32[]{:S(2)}, u32[]{:S(2)}) collective-permute-start(bf16[32,512]{1,0:T(8,128)(2,1)} %param.3), channel_id=1, source_target_pairs={{0,1},{1,0},{2,3},{3,2},{4,5},{5,4},{6,7},{7,6},{8,9},{9,8},{10,11... | collective-permute-start | bytes 98312 | tf_op jit(solution)/shard_map/ppermute | solution.py:39
  0.5 0.8 %constant_dynamic-update-slice_fusion.2 = bf16[128,512]{1,0:T(8,128)(2,1)S(1)} fusion(bf16[32,512]{1,0:T(8,128)(2,1)} %param.3), kind=kLoop, calls=%fused_computation.31 | loop fusion | bytes 65536
  1.2 0.3 collective-permute-done
  1.5 2.9 %collective-permute-start.1 = (bf16[64,512]{1,0:T(8,128)(2,1)S(1)}, bf16[64,512]{1,0:T(8,128)(2,1)S(1)}, u32[]{:S(2)}, u32[]{:S(2)}) collective-permute-start(bf16[64,512]{1,0:T(8,128)(2,1)S(1)} %pad_maximum_fusion), channel_id=1, source_target_pairs={{0,2},{1,3},{2,0},{3,1},{4,6},{5,7},{6,4},{7,5},{8,10},{9,11},{10,... | collective-permute-start | bytes 196616 | tf_op jit(solution)/shard_map/ppermute | solution.py:33
  4.5 2.4 %collective-permute-done.1 = bf16[64,512]{1,0:T(8,128)(2,1)S(1)} collective-permute-done((bf16[64,512]{1,0:T(8,128)(2,1)S(1)}, bf16[64,512]{1,0:T(8,128)(2,1)S(1)}, u32[]{:S(2)}, u32[]{:S(2)}) %collective-permute-start.1) | collective-permute-done | bytes 65568 | tf_op jit(solution)/shard_map/ppermute | solution.py:33
  6.9 0.7 %collective-permute-start.2 = (bf16[128,512]{1,0:T(8,128)(2,1)S(1)}, bf16[128,512]{1,0:T(8,128)(2,1)S(1)}, u32[]{:S(2)}, u32[]{:S(2)}) collective-permute-start(bf16[128,512]{1,0:T(8,128)(2,1)S(1)} %constant_dynamic-update-slice_fusion), channel_id=1, source_target_pairs={{0,0},{1,5},{2,2},{3,7},{4,4},{5,1},{6,6},{7,3},{8,8},{9,13},{10,1... | collective-permute-start | bytes 393224 | tf_op jit(solution)/shard_map/ppermute | solution.py:33
  7.6 4.0 %collective-permute-start.3 = (bf16[128,512]{1,0:T(8,128)(2,1)S(1)}, bf16[128,512]{1,0:T(8,128)(2,1)S(1)}, u32[]{:S(2)}, u32[]{:S(2)}) collective-permute-start(bf16[128,512]{1,0:T(8,128)(2,1)S(1)} %constant_dynamic-update-slice_fusion), channel_id=1, source_target_pairs={{0,12},{1,9},{2,14},{3,11},{4,8},{5,13},{6,10},{7,15},{8,4},{9,1},... | collective-permute-start | bytes 393224 | tf_op jit(solution)/shard_map/ppermute | solution.py:33
  11.6 1.2 %multiply_reduce_fusion = f32[512]{0:T(512)S(1)} fusion(bf16[512,512]{1,0:T(8,128)(2,1)} %param.4), kind=kLoop, calls=%fused_computation.8 | loop fusion | flops 785920 | bytes 526336 | tf_op jit(solution)/shard_map/reduce_sum | solution.py:37
  12.8 3.0 %collective-permute-done.3 = bf16[128,512]{1,0:T(8,128)(2,1)S(1)} collective-permute-done((bf16[128,512]{1,0:T(8,128)(2,1)S(1)}, bf16[128,512]{1,0:T(8,128)(2,1)S(1)}, u32[]{:S(2)}, u32[]{:S(2)}) %collective-permute-start.3) | collective-permute-done | bytes 131104 | tf_op jit(solution)/shard_map/ppermute | solution.py:33
  15.8 0.1 multiply_reduce_fusion.1
  16.0 1.5 %convolution_convert_fusion = bf16[256,1024]{1,0:T(8,128)(2,1)} fusion(bf16[512,1024]{1,0:T(8,128)(2,1)S(1)} %copy-done, bf16[256,512]{1,0:T(8,128)(2,1)S(1)} %constant_dynamic-update-slice_fusion.3, bf16[512,512]{1,0:T(8,128)(2,1)S(1)} %copy-done.1, f32[256]{0:T(256)S(1)} %multiply_reduce_fusion.1, f32[512]{0:T(512)S(1)} %multiply_reduce_fusion), kind=kOutput, calls=%fused_computation | convolution fusion | flops 403570688 | bytes 2362368 | tf_op jit(solution)/shard_map/dot_general | solution.py:16
  17.5 2.2 %collective-permute-start.5 = (bf16[256,1024]{1,0:T(8,128)(2,1)}, bf16[256,1024]{1,0:T(8,128)(2,1)S(1)}, u32[]{:S(2)}, u32[]{:S(2)}) collective-permute-start(bf16[256,1024]{1,0:T(8,128)(2,1)} %convolution_convert_fusion), channel_id=1, source_target_pairs={{0,1},{1,0},{2,3},{3,2},{4,5},{5,4},{6,7},{7,6},{8,9},{9,8},{10,11... | collective-permute-start | bytes 1572872 | tf_op jit(solution)/shard_map/ppermute | solution.py:47
  19.6 1.8 %collective-permute-done.4 = bf16[256,512]{1,0:T(8,128)(2,1)S(1)} collective-permute-done((bf16[256,512]{1,0:T(8,128)(2,1)S(1)}, bf16[256,512]{1,0:T(8,128)(2,1)S(1)}, u32[]{:S(2)}, u32[]{:S(2)}) %collective-permute-start.4) | collective-permute-done | bytes 262176 | tf_op jit(solution)/shard_map/ppermute | solution.py:44
  21.4 0.1 multiply_reduce_fusion.2
  21.6 0.2 collective-permute-done.5
  21.8 0.7 %add_convert_fusion = bf16[256,1024]{1,0:T(8,128)(2,1)S(1)} fusion(bf16[256,1024]{1,0:T(8,128)(2,1)S(1)} %collective-permute-done.5, bf16[512,1024]{1,0:T(8,128)(2,1)S(1)} %copy-done, bf16[256,512]{1,0:T(8,128)(2,1)S(1)} %collective-permute-done.4, bf16[512,512]{1,0:T(8,128)(2,1)S(1)} %copy-done.1, f32[512]{0:T(512)S(1)} %multiply_reduce_fusion, ...), kind=kOutput, calls=%fused_computation.7 | convolution fusion | flops 404094976 | bytes 2886656 | tf_op jit(solution)/shard_map/dot_general | solution.py:16
  22.5 2.8 %collective-permute-start.6 = (bf16[64,1024]{1,0:T(8,128)(2,1)S(1)}, bf16[64,1024]{1,0:T(8,128)(2,1)S(1)}, u32[]{:S(2)}, u32[]{:S(2)}) collective-permute-start(bf16[64,1024]{1,0:T(8,128)(2,1)S(1)} %get-tuple-element.5), channel_id=1, source_target_pairs={{0,10},{1,15},{2,8},{3,13},{4,14},{5,11},{6,12},{7,9},{8,2},{9,7},... | collective-permute-start | bytes 393224 | tf_op jit(solution)/shard_map/ppermute | solution.py:33
  25.3 1.2 %collective-permute-start.7 = (bf16[64,1024]{1,0:T(8,128)(2,1)S(1)}, bf16[64,1024]{1,0:T(8,128)(2,1)S(1)}, u32[]{:S(2)}, u32[]{:S(2)}) collective-permute-start(bf16[64,1024]{1,0:T(8,128)(2,1)S(1)} %get-tuple-element.8), channel_id=1, source_target_pairs={{0,8},{1,13},{2,10},{3,15},{4,12},{5,9},{6,14},{7,11},{8,0},{9,5},... | collective-permute-start | bytes 393224 | tf_op jit(solution)/shard_map/ppermute | solution.py:33
  26.5 0.7 %collective-permute-start.8 = (bf16[64,1024]{1,0:T(8,128)(2,1)S(1)}, bf16[64,1024]{1,0:T(8,128)(2,1)S(1)}, u32[]{:S(2)}, u32[]{:S(2)}) collective-permute-start(bf16[64,1024]{1,0:T(8,128)(2,1)S(1)} %get-tuple-element.7), channel_id=1, source_target_pairs={{0,6},{1,3},{2,4},{3,1},{4,2},{5,7},{6,0},{7,5},{8,14},{9,11},{10,... | collective-permute-start | bytes 393224 | tf_op jit(solution)/shard_map/ppermute | solution.py:33
  27.2 3.2 %collective-permute-start.9 = (bf16[64,1024]{1,0:T(8,128)(2,1)S(1)}, bf16[64,1024]{1,0:T(8,128)(2,1)S(1)}, u32[]{:S(2)}, u32[]{:S(2)}) collective-permute-start(bf16[64,1024]{1,0:T(8,128)(2,1)S(1)} %get-tuple-element.6), channel_id=1, source_target_pairs={{0,4},{1,1},{2,6},{3,3},{4,0},{5,5},{6,2},{7,7},{8,12},{9,9},{10,1... | collective-permute-start | bytes 393224 | tf_op jit(solution)/shard_map/ppermute | solution.py:33
  30.4 5.9 %collective-permute-done.6 = bf16[64,1024]{1,0:T(8,128)(2,1)S(1)} collective-permute-done((bf16[64,1024]{1,0:T(8,128)(2,1)S(1)}, bf16[64,1024]{1,0:T(8,128)(2,1)S(1)}, u32[]{:S(2)}, u32[]{:S(2)}) %collective-permute-start.6) | collective-permute-done | bytes 131104 | tf_op jit(solution)/shard_map/ppermute | solution.py:33
  36.2 1.4 %collective-permute-done.7 = bf16[64,1024]{1,0:T(8,128)(2,1)S(1)} collective-permute-done((bf16[64,1024]{1,0:T(8,128)(2,1)S(1)}, bf16[64,1024]{1,0:T(8,128)(2,1)S(1)}, u32[]{:S(2)}, u32[]{:S(2)}) %collective-permute-start.7) | collective-permute-done | bytes 131104 | tf_op jit(solution)/shard_map/ppermute | solution.py:33
  37.9 1.3 %collective-permute-done.10 = f32[32,1024]{1,0:T(8,128)S(1)} collective-permute-done((f32[32,1024]{1,0:T(8,128)S(1)}, f32[32,1024]{1,0:T(8,128)S(1)}, u32[]{:S(2)}, u32[]{:S(2)}) %collective-permute-start.10) | collective-permute-done | bytes 131104 | tf_op jit(solution)/shard_map/ppermute | solution.py:58
  39.2 0.7 %slice_add_fusion = f32[32,1024]{1,0:T(8,128)} fusion(f32[32,1024]{1,0:T(8,128)S(1)} %collective-permute-done.10, f32[64,1024]{1,0:T(8,128)S(1)} %convert_add_fusion), kind=kLoop, calls=%fused_computation.23 | loop fusion | flops 32768 | bytes 393216 | tf_op jit(solution)/shard_map/add | solution.py:58
  (19 shorter events, 0.2 us)
Async XLA Ops:
  0.0 16.0 %copy-start = (bf16[512,1024]{1,0:T(8,128)(2,1)S(1)}, bf16[512,1024]{1,0:T(8,128)(2,1)}, u32[]{:S(2)}) copy-start(bf16[512,1024]{1,0:T(8,128)(2,1)} %param.5) | copy-start | bytes 3145732
  0.0 1.5 %copy-start.2 = (bf16[32,512]{1,0:T(8,128)(2,1)S(1)}, bf16[32,512]{1,0:T(8,128)(2,1)}, u32[]{:S(2)}) copy-start(bf16[32,512]{1,0:T(8,128)(2,1)} %param.3) | copy-start | bytes 98308
  0.0 1.5 %collective-permute-start = (bf16[32,512]{1,0:T(8,128)(2,1)}, bf16[32,512]{1,0:T(8,128)(2,1)S(1)}, u32[]{:S(2)}, u32[]{:S(2)}) collective-permute-start(bf16[32,512]{1,0:T(8,128)(2,1)} %param.3), channel_id=1, source_target_pairs={{0,1},{1,0},{2,3},{3,2},{4,5},{5,4},{6,7},{7,6},{8,9},{9,8},{10,11... | collective-permute-start | bytes 98312 | tf_op jit(solution)/shard_map/ppermute | solution.py:39
  1.5 5.3 %collective-permute-start.1 = (bf16[64,512]{1,0:T(8,128)(2,1)S(1)}, bf16[64,512]{1,0:T(8,128)(2,1)S(1)}, u32[]{:S(2)}, u32[]{:S(2)}) collective-permute-start(bf16[64,512]{1,0:T(8,128)(2,1)S(1)} %pad_maximum_fusion), channel_id=1, source_target_pairs={{0,2},{1,3},{2,0},{3,1},{4,6},{5,7},{6,4},{7,5},{8,10},{9,11},{10,... | collective-permute-start | bytes 196616 | tf_op jit(solution)/shard_map/ppermute | solution.py:33
  6.9 5.9 %collective-permute-start.2 = (bf16[128,512]{1,0:T(8,128)(2,1)S(1)}, bf16[128,512]{1,0:T(8,128)(2,1)S(1)}, u32[]{:S(2)}, u32[]{:S(2)}) collective-permute-start(bf16[128,512]{1,0:T(8,128)(2,1)S(1)} %constant_dynamic-update-slice_fusion), channel_id=1, source_target_pairs={{0,0},{1,5},{2,2},{3,7},{4,4},{5,1},{6,6},{7,3},{8,8},{9,13},{10,1... | collective-permute-start | bytes 393224 | tf_op jit(solution)/shard_map/ppermute | solution.py:33
  7.6 8.3 %collective-permute-start.3 = (bf16[128,512]{1,0:T(8,128)(2,1)S(1)}, bf16[128,512]{1,0:T(8,128)(2,1)S(1)}, u32[]{:S(2)}, u32[]{:S(2)}) collective-permute-start(bf16[128,512]{1,0:T(8,128)(2,1)S(1)} %constant_dynamic-update-slice_fusion), channel_id=1, source_target_pairs={{0,12},{1,9},{2,14},{3,11},{4,8},{5,13},{6,10},{7,15},{8,4},{9,1},... | collective-permute-start | bytes 393224 | tf_op jit(solution)/shard_map/ppermute | solution.py:33
  12.8 3.2 %copy-start.1 = (bf16[512,512]{1,0:T(8,128)(2,1)S(1)}, bf16[512,512]{1,0:T(8,128)(2,1)}, u32[]{:S(2)}) copy-start(bf16[512,512]{1,0:T(8,128)(2,1)} %param.4) | copy-start | bytes 1572868
  17.5 4.3 %collective-permute-start.5 = (bf16[256,1024]{1,0:T(8,128)(2,1)}, bf16[256,1024]{1,0:T(8,128)(2,1)S(1)}, u32[]{:S(2)}, u32[]{:S(2)}) collective-permute-start(bf16[256,1024]{1,0:T(8,128)(2,1)} %convolution_convert_fusion), channel_id=1, source_target_pairs={{0,1},{1,0},{2,3},{3,2},{4,5},{5,4},{6,7},{7,6},{8,9},{9,8},{10,11... | collective-permute-start | bytes 1572872 | tf_op jit(solution)/shard_map/ppermute | solution.py:47
  19.6 1.8 %collective-permute-start.4 = (bf16[256,512]{1,0:T(8,128)(2,1)S(1)}, bf16[256,512]{1,0:T(8,128)(2,1)S(1)}, u32[]{:S(2)}, u32[]{:S(2)}) collective-permute-start(bf16[256,512]{1,0:T(8,128)(2,1)S(1)} %constant_dynamic-update-slice_fusion.3), channel_id=1, source_target_pairs={{0,1},{1,0},{2,3},{3,2},{4,5},{5,4},{6,7},{7,6},{8,9},{9,8},{10,11... | collective-permute-start | bytes 786440 | tf_op jit(solution)/shard_map/ppermute | solution.py:44
  22.5 13.7 %collective-permute-start.6 = (bf16[64,1024]{1,0:T(8,128)(2,1)S(1)}, bf16[64,1024]{1,0:T(8,128)(2,1)S(1)}, u32[]{:S(2)}, u32[]{:S(2)}) collective-permute-start(bf16[64,1024]{1,0:T(8,128)(2,1)S(1)} %get-tuple-element.5), channel_id=1, source_target_pairs={{0,10},{1,15},{2,8},{3,13},{4,14},{5,11},{6,12},{7,9},{8,2},{9,7},... | collective-permute-start | bytes 393224 | tf_op jit(solution)/shard_map/ppermute | solution.py:33
  25.3 12.4 %collective-permute-start.7 = (bf16[64,1024]{1,0:T(8,128)(2,1)S(1)}, bf16[64,1024]{1,0:T(8,128)(2,1)S(1)}, u32[]{:S(2)}, u32[]{:S(2)}) collective-permute-start(bf16[64,1024]{1,0:T(8,128)(2,1)S(1)} %get-tuple-element.8), channel_id=1, source_target_pairs={{0,8},{1,13},{2,10},{3,15},{4,12},{5,9},{6,14},{7,11},{8,0},{9,5},... | collective-permute-start | bytes 393224 | tf_op jit(solution)/shard_map/ppermute | solution.py:33
  26.5 11.2 %collective-permute-start.8 = (bf16[64,1024]{1,0:T(8,128)(2,1)S(1)}, bf16[64,1024]{1,0:T(8,128)(2,1)S(1)}, u32[]{:S(2)}, u32[]{:S(2)}) collective-permute-start(bf16[64,1024]{1,0:T(8,128)(2,1)S(1)} %get-tuple-element.7), channel_id=1, source_target_pairs={{0,6},{1,3},{2,4},{3,1},{4,2},{5,7},{6,0},{7,5},{8,14},{9,11},{10,... | collective-permute-start | bytes 393224 | tf_op jit(solution)/shard_map/ppermute | solution.py:33
  27.2 10.5 %collective-permute-start.9 = (bf16[64,1024]{1,0:T(8,128)(2,1)S(1)}, bf16[64,1024]{1,0:T(8,128)(2,1)S(1)}, u32[]{:S(2)}, u32[]{:S(2)}) collective-permute-start(bf16[64,1024]{1,0:T(8,128)(2,1)S(1)} %get-tuple-element.6), channel_id=1, source_target_pairs={{0,4},{1,1},{2,6},{3,3},{4,0},{5,5},{6,2},{7,7},{8,12},{9,9},{10,1... | collective-permute-start | bytes 393224 | tf_op jit(solution)/shard_map/ppermute | solution.py:33
  37.8 1.4 %collective-permute-start.10 = (f32[32,1024]{1,0:T(8,128)S(1)}, f32[32,1024]{1,0:T(8,128)S(1)}, u32[]{:S(2)}, u32[]{:S(2)}) collective-permute-start(f32[32,1024]{1,0:T(8,128)S(1)} %slice.29), channel_id=1, source_target_pairs={{0,1},{1,0},{2,3},{3,2},{4,5},{5,4},{6,7},{7,6},{8,9},{9,8},{10,11... | collective-permute-start | bytes 393224 | tf_op jit(solution)/shard_map/ppermute | solution.py:58

commit v2 on v0

v2 whole, which is shorter than its diff:
```python
import jax
import jax.numpy as jnp
from jax import lax
from jax.experimental import pallas as pl
from jax.experimental.pallas import tpu as pltpu
from jax.sharding import PartitionSpec as P

AXES = ("lm", "env")
HEAVY = 10**11
VMEM = pl.BlockSpec(memory_space=pltpu.VMEM)
PARAMS = pltpu.CompilerParams(vmem_limit_bytes=16 * 2**20)


def load_body(landmarks, weights, landmarks_out, weights_out, land_sq, sems):
    first = pltpu.make_async_copy(landmarks, landmarks_out, sems.at[0])
    second = pltpu.make_async_copy(weights, weights_out, sems.at[1])
    first.start()
    second.start()
    first.wait()
    square = jnp.square(landmarks_out[...].astype(jnp.float32))
    land_sq[...] = lax.dot_general(
        jnp.ones((8, square.shape[1]), jnp.float32),
        square,
        (((1,), (1,)), ((), ())),
        precision=lax.Precision.HIGHEST,
        preferred_element_type=jnp.float32,
    )
    second.wait()


def load(landmarks, weights):
    return pl.pallas_call(
        load_body,
        out_shape=[
            jax.ShapeDtypeStruct(landmarks.shape, landmarks.dtype),
            jax.ShapeDtypeStruct(weights.shape, weights.dtype),
            jax.ShapeDtypeStruct((8, landmarks.shape[0]), jnp.float32),
        ],
        in_specs=[pl.BlockSpec(memory_space=pltpu.HBM)] * 2,
        out_specs=[VMEM] * 3,
        scratch_shapes=[pltpu.SemaphoreType.DMA((2,))],
        compiler_params=PARAMS,
        cost_estimate=pl.CostEstimate(flops=10**9, bytes_accessed=0, transcendentals=0),
    )(*[pltpu.with_memory_space_constraint(x, pltpu.HBM) for x in (landmarks, weights)])


def kernel_sums(rows, landmarks, land_sq, weights):
    row_sq = jnp.sum(jnp.square(rows.astype(jnp.float32)), axis=1, keepdims=True)
    cross = lax.dot_general(
        rows, landmarks, (((1,), (1,)), ((), ())), preferred_element_type=jnp.float32
    )
    dist = row_sq + land_sq - 2.0 * cross
    kern = jnp.exp(-(4.0 / rows.shape[1]) * dist).astype(jnp.bfloat16)
    return jnp.dot(kern, weights, preferred_element_type=jnp.float32)


def give_body(rows, landmarks, land_sq, weights, out):
    sums = kernel_sums(rows[...], landmarks[...], land_sq[0:1], weights[...])
    out[...] = sums.astype(out.dtype)


def keep_body(rows, landmarks, land_sq, weights, taken, *outs):
    sums = kernel_sums(rows[...], landmarks[...], land_sq[0:1], weights[...])
    sums += taken[...].astype(jnp.float32)
    at = 0
    for out in outs:
        out[...] = sums[at : at + out.shape[0]].astype(out.dtype)
        at += out.shape[0]


def add_body(*refs):
    *parts, out = refs
    total = parts[0][...].astype(jnp.float32)
    for part in parts[1:]:
        total += part[...].astype(jnp.float32)
    out[...] = total


def add(*parts, weight=1):
    return pl.pallas_call(
        add_body,
        out_shape=jax.ShapeDtypeStruct(parts[0].shape, jnp.float32),
        in_specs=[VMEM] * len(parts),
        out_specs=VMEM,
        compiler_params=PARAMS,
        cost_estimate=pl.CostEstimate(
            flops=weight * HEAVY, bytes_accessed=0, transcendentals=0
        ),
    )(*parts)


def call(body, sizes, *args, rounds=1):
    rows, landmarks, _, weights = args[:4]
    read = sum(arg.size * arg.dtype.itemsize for arg in args)
    cost = pl.CostEstimate(
        flops=rounds * 2 * rows.shape[0] * landmarks.shape[0] * (rows.shape[1] + weights.shape[1]),
        bytes_accessed=rounds * read,
        transcendentals=rows.shape[0] * landmarks.shape[0],
    )
    return pl.pallas_call(
        body,
        out_shape=[jax.ShapeDtypeStruct((size, weights.shape[1]), jnp.bfloat16) for size in sizes],
        in_specs=[VMEM] * len(args),
        out_specs=[VMEM] * len(sizes),
        compiler_params=PARAMS,
        cost_estimate=cost,
    )(*args)


def solution(mesh):
    chips = mesh.shape["lm"]
    inner = 1 << ((chips.bit_length() - 1) // 2)
    outer = chips // inner
    steps = ([0] + list(range(outer - 1, outer // 2, -1)), list(range(1, outer // 2 + 1)))

    def exchange(block, by, cross=0):
        pairs = [
            (2 * chip + core, 2 * (chip ^ by[core]) + (core ^ cross))
            for chip in range(chips)
            for core in range(2)
        ]
        return lax.ppermute(block, AXES, pairs)

    def swap(block):
        return exchange(block, (0, 0), 1)

    def local(env_desc, landmarks, whitening):
        rows = env_desc.shape[0]

        chip_rows = jnp.concatenate([env_desc, swap(env_desc)])
        landmarks, chip_rows = lax.optimization_barrier((landmarks, chip_rows))
        got = [exchange(chip_rows, (a * inner, b * inner)) for a, b in reversed(list(zip(*steps)))]
        landmarks, whitening, land_sq = load(landmarks, whitening)
        got, land_sq = lax.optimization_barrier((got, land_sq))
        got = jnp.concatenate(got[::-1])
        lines = [got] + [exchange(got, (k, k)) for k in range(1, inner)]

        tables = (landmarks, land_sq, whitening)
        given = [
            call(give_body, [first.shape[0]], first, *tables, rounds=20 if k else 1)[0]
            for k, first in enumerate(lines)
        ]
        taken = [swap(given[0])]
        taken[0], *given[1:] = lax.optimization_barrier(taken + given[1:])
        taken += [swap(block) for block in given[1:]]
        parts = []
        for k, first in enumerate(lines):
            sizes = [2 * rows] * (outer // 2)
            if k == inner - 1:
                sizes[-1:] = [rows, rows]
            blocks = call(keep_body, sizes, swap(first), *tables, taken[k])
            for i in reversed(range(outer // 2)):
                by = (steps[1][i] * inner + k, steps[0][i] * inner + k)
                if k == inner - 1 and i == outer // 2 - 1:
                    last = [exchange(blocks[-1], by), exchange(blocks[-2], by, 1)]
                else:
                    parts.append(exchange(blocks[i], by))
        total = add(*parts)
        return add(total[rows:], *last) + swap(total[:rows])

    return jax.shard_map(
        local,
        mesh=mesh,
        in_specs=(P(("group", "lm", "env"), None), P(("lm", "env"), None), P(("lm", "env"), None)),
        out_specs=P(("group", "lm", "env"), None),
        check_vma=False,
    )
```

time: 102 us -> 36.2 us (0.35)
  the two profiles are of different devices: /device:TPU:0 before, /device:TPU:1 now
where the time goes in v2:
time: 36.2 us; the launch traced here: 36 us
  starting transfers between devices  22.2 us (61%)
  waiting for transfers between devices  7.69 us (21%)
  Pallas kernels  4.42 us (12%)
  other arithmetic  1.43 us (4%)
    ppermute x14, starting transfers between devices, exchange(): return lax.ppermute(block, AXES, pairs)  22.2 us
    ppermute x14, waiting for transfers between devices, exchange(): return lax.ppermute(block, AXES, pairs)  7.69 us
    pallas_call x4, Pallas kernels, call(): pl.pallas_call(body, out_shape=[jax.ShapeDtypeStruct((size, weights.shape...  2.34 us
    pallas_call x1, Pallas kernels, load(): pl.pallas_call(load_body, out_shape=[jax.ShapeDtypeStruct(landmarks.shape...  2 us
    concatenate x1, other arithmetic, local(): chip_rows = jnp.concatenate([env_desc, swap(env_desc)])  0.76 us
  transfers between devices with their start and end apart: 14, of which 4 were waited for; matrix products, arithmetic and copies ran while one was open for 0% of the time, Pallas kernels for 12%

profile of v2, /device:TPU:1, one launch (start us, length us, event | category | flops | bytes accessed | tf_op | source)
XLA Modules:
  0.0 36.0 jit_solution(3671240515131391892)
XLA Ops:
  0.1 1.4 %collective-permute-done = bf16[32,512]{1,0:T(8,128)(2,1)S(1)} collective-permute-done((bf16[32,512]{1,0:T(8,128)(2,1)}, bf16[32,512]{1,0:T(8,128)(2,1)S(1)}, u32[]{:S(2)}, u32[]{:S(2)}) %collective-permute-start) | collective-permute-done | bytes 32800 | tf_op jit(solution)/shard_map/ppermute | solution.py:122
  1.4 0.8 %pad_maximum_fusion = bf16[64,512]{1,0:T(8,128)(2,1)S(1)} fusion(bf16[32,512]{1,0:T(8,128)(2,1)S(1)} %collective-permute-done, bf16[32,512]{1,0:T(8,128)(2,1)} %param.3), kind=kLoop, calls=%fused_computation | loop fusion | flops 131072 | bytes 131072 | tf_op jit(solution)/shard_map/concatenate | solution.py:130
  2.2 3.5 %collective-permute-start.1 = (bf16[64,512]{1,0:T(8,128)(2,1)S(1)}, bf16[64,512]{1,0:T(8,128)(2,1)S(1)}, u32[]{:S(2)}, u32[]{:S(2)}) collective-permute-start(bf16[64,512]{1,0:T(8,128)(2,1)S(1)} %pad_maximum_fusion), channel_id=1, source_target_pairs={{0,12},{1,9},{2,14},{3,11},{4,8},{5,13},{6,10},{7,15},{8,4},{9,1},... | collective-permute-start | bytes 196616 | tf_op jit(solution)/shard_map/ppermute | solution.py:122
  5.6 3.2 %collective-permute-start.2 = (bf16[64,512]{1,0:T(8,128)(2,1)S(1)}, bf16[64,512]{1,0:T(8,128)(2,1)S(1)}, u32[]{:S(2)}, u32[]{:S(2)}) collective-permute-start(bf16[64,512]{1,0:T(8,128)(2,1)S(1)} %pad_maximum_fusion), channel_id=1, source_target_pairs={{0,0},{1,5},{2,2},{3,7},{4,4},{5,1},{6,6},{7,3},{8,8},{9,13},{10,1... | collective-permute-start | bytes 196616 | tf_op jit(solution)/shard_map/ppermute | solution.py:122
  8.8 2.0 %shard_map.37 = (bf16[512,512]{1,0:T(8,128)(2,1)S(1)}, bf16[512,1024]{1,0:T(8,128)(2,1)S(1)}, f32[8,512]{1,0:T(8,128)S(1)}) custom-call(bf16[512,512]{1,0:T(8,128)(2,1)} %landmarks, bf16[512,1024]{1,0:T(8,128)(2,1)} %weights.1), custom_call_target="tpu_custom_call" | custom-call | flops 1000000000 | tf_op jit(solution)/shard_map/pallas_call | solution.py:32
  10.9 1.3 %collective-permute-start.5 = (bf16[128,512]{1,0:T(8,128)(2,1)S(1)}, bf16[128,512]{1,0:T(8,128)(2,1)S(1)}, u32[]{:S(2)}, u32[]{:S(2)}) collective-permute-start(bf16[128,512]{1,0:T(8,128)(2,1)S(1)} %constant_dynamic-update-slice_fusion.rows), channel_id=1, source_target_pairs={{0,2},{1,3},{2,0},{3,1},{4,6},{5,7},{6,4},{7,5},{8,10},{9,11},{10,... | collective-permute-start | bytes 393224 | tf_op jit(solution)/shard_map/ppermute | solution.py:122
  12.2 0.6 %shard_map.38 = bf16[128,1024]{1,0:T(8,128)(2,1)S(1)} custom-call(bf16[128,512]{1,0:T(8,128)(2,1)S(1)} %constant_dynamic-update-slice_fusion.rows, bf16[512,512]{1,0:T(8,128)(2,1)S(1)} %get-tuple-element.25.landmarks, f32[8,512]{1,0:T(8,128)S(1)} %get-tuple-element.26.land_sq, bf16[512,1024]{1,0:T(8,128)(2,1)S(1)} %get-tuple-element.27.weights), custom_call_target="tpu_custom_call" | custom-call | flops 201326592 | bytes 1720320 | tf_op jit(solution)/shard_map/pallas_call | solution.py:100
  12.8 0.1 collective-permute-start.4
  12.9 2.9 %collective-permute-done.5.rows = bf16[128,512]{1,0:T(8,128)(2,1)S(1)} collective-permute-done((bf16[128,512]{1,0:T(8,128)(2,1)S(1)}, bf16[128,512]{1,0:T(8,128)(2,1)S(1)}, u32[]{:S(2)}, u32[]{:S(2)}) %collective-permute-start.5) | collective-permute-done | bytes 131104 | tf_op jit(solution)/shard_map/ppermute | solution.py:122
  15.8 0.6 %shard_map.39 = bf16[128,1024]{1,0:T(8,128)(2,1)S(1)} custom-call(bf16[128,512]{1,0:T(8,128)(2,1)S(1)} %collective-permute-done.5.rows, bf16[512,512]{1,0:T(8,128)(2,1)S(1)} %get-tuple-element.25.landmarks, f32[8,512]{1,0:T(8,128)S(1)} %get-tuple-element.26.land_sq, bf16[512,1024]{1,0:T(8,128)(2,1)S(1)} %get-tuple-element.27.weights), custom_call_target="tpu_custom_call" | custom-call | flops 4026531840 | bytes 34406400 | tf_op jit(solution)/shard_map/pallas_call | solution.py:100
  16.4 0.4 %collective-permute-start.9 = (bf16[128,1024]{1,0:T(8,128)(2,1)S(1)}, bf16[128,1024]{1,0:T(8,128)(2,1)S(1)}, u32[]{:S(2)}, u32[]{:S(2)}) collective-permute-start(bf16[128,1024]{1,0:T(8,128)(2,1)S(1)} %shard_map.39), channel_id=1, source_target_pairs={{0,1},{1,0},{2,3},{3,2},{4,5},{5,4},{6,7},{7,6},{8,9},{9,8},{10,11... | collective-permute-start | bytes 786440 | tf_op jit(solution)/shard_map/ppermute | solution.py:122
  16.8 0.2 collective-permute-start.3
  16.9 0.3 collective-permute-start.8
  17.3 0.9 %collective-permute-done.3.rows = bf16[128,512]{1,0:T(8,128)(2,1)S(1)} collective-permute-done((bf16[128,512]{1,0:T(8,128)(2,1)S(1)}, bf16[128,512]{1,0:T(8,128)(2,1)S(1)}, u32[]{:S(2)}, u32[]{:S(2)}) %collective-permute-start.3) | collective-permute-done | bytes 131104 | tf_op jit(solution)/shard_map/ppermute | solution.py:122
  18.2 0.6 %shard_map.40 = (bf16[64,1024]{1,0:T(8,128)(2,1)S(1)}, bf16[64,1024]{1,0:T(8,128)(2,1)S(1)}) custom-call(bf16[128,512]{1,0:T(8,128)(2,1)S(1)} %collective-permute-done.3.rows, bf16[512,512]{1,0:T(8,128)(2,1)S(1)} %get-tuple-element.25.landmarks, f32[8,512]{1,0:T(8,128)S(1)} %get-tuple-element.26.land_sq, bf16[512,1024]{1,0:T(8,128)(2,1)S(1)} %get-tuple-element.27.weights, ...), custom_call_target="tpu_custom_call" | custom-call | flops 201326592 | bytes 1982464 | tf_op jit(solution)/shard_map/pallas_call | solution.py:100
  18.7 2.9 %collective-permute-start.6 = (bf16[64,1024]{1,0:T(8,128)(2,1)S(1)}, bf16[64,1024]{1,0:T(8,128)(2,1)S(1)}, u32[]{:S(2)}, u32[]{:S(2)}) collective-permute-start(bf16[64,1024]{1,0:T(8,128)(2,1)S(1)} %get-tuple-element.29), channel_id=1, source_target_pairs={{0,8},{1,13},{2,10},{3,15},{4,12},{5,9},{6,14},{7,11},{8,0},{9,5},... | collective-permute-start | bytes 393224 | tf_op jit(solution)/shard_map/ppermute | solution.py:122
  21.6 0.7 %collective-permute-start.7 = (bf16[64,1024]{1,0:T(8,128)(2,1)S(1)}, bf16[64,1024]{1,0:T(8,128)(2,1)S(1)}, u32[]{:S(2)}, u32[]{:S(2)}) collective-permute-start(bf16[64,1024]{1,0:T(8,128)(2,1)S(1)} %get-tuple-element.30), channel_id=1, source_target_pairs={{0,4},{1,1},{2,6},{3,3},{4,0},{5,5},{6,2},{7,7},{8,12},{9,9},{10,1... | collective-permute-start | bytes 393224 | tf_op jit(solution)/shard_map/ppermute | solution.py:122
  22.3 0.6 %shard_map.41 = (bf16[64,1024]{1,0:T(8,128)(2,1)S(1)}, bf16[32,1024]{1,0:T(8,128)(2,1)S(1)}, bf16[32,1024]{1,0:T(8,128)(2,1)S(1)}) custom-call(bf16[128,512]{1,0:T(8,128)(2,1)S(1)} %collective-permute-done.8.rows, bf16[512,512]{1,0:T(8,128)(2,1)S(1)} %get-tuple-element.25.landmarks, f32[8,512]{1,0:T(8,128)S(1)} %get-tuple-element.26.land_sq, ...), custom_call_target="tpu_custom_call" | custom-call | flops 201326592 | bytes 1982464 | tf_op jit(solution)/shard_map/pallas_call | solution.py:100
  22.9 1.3 %collective-permute-start.10 = (bf16[64,1024]{1,0:T(8,128)(2,1)S(1)}, bf16[64,1024]{1,0:T(8,128)(2,1)S(1)}, u32[]{:S(2)}, u32[]{:S(2)}) collective-permute-start(bf16[64,1024]{1,0:T(8,128)(2,1)S(1)} %get-tuple-element.32), channel_id=1, source_target_pairs={{0,6},{1,3},{2,4},{3,1},{4,2},{5,7},{6,0},{7,5},{8,14},{9,11},{10,... | collective-permute-start | bytes 393224 | tf_op jit(solution)/shard_map/ppermute | solution.py:122
  24.2 0.4 %collective-permute-start.11 = (bf16[32,1024]{1,0:T(8,128)(2,1)S(1)}, bf16[32,1024]{1,0:T(8,128)(2,1)S(1)}, u32[]{:S(2)}, u32[]{:S(2)}) collective-permute-start(bf16[32,1024]{1,0:T(8,128)(2,1)S(1)} %get-tuple-element.33), channel_id=1, source_target_pairs={{0,10},{1,15},{2,8},{3,13},{4,14},{5,11},{6,12},{7,9},{8,2},{9,7},... | collective-permute-start | bytes 196616 | tf_op jit(solution)/shard_map/ppermute | solution.py:122
  24.6 6.7 %collective-permute-start.12 = (bf16[32,1024]{1,0:T(8,128)(2,1)S(1)}, bf16[32,1024]{1,0:T(8,128)(2,1)S(1)}, u32[]{:S(2)}, u32[]{:S(2)}) collective-permute-start(bf16[32,1024]{1,0:T(8,128)(2,1)S(1)} %get-tuple-element.34), channel_id=1, source_target_pairs={{0,11},{1,14},{2,9},{3,12},{4,15},{5,10},{6,13},{7,8},{8,3},{9,6},... | collective-permute-start | bytes 196616 | tf_op jit(solution)/shard_map/ppermute | solution.py:122
  31.4 1.3 %collective-permute-start.13 = (f32[32,1024]{1,0:T(8,128)S(1)}, f32[32,1024]{1,0:T(8,128)S(1)}, u32[]{:S(2)}, u32[]{:S(2)}) collective-permute-start(f32[32,1024]{1,0:T(8,128)S(1)} %get-tuple-element.35), channel_id=1, source_target_pairs={{0,1},{1,0},{2,3},{3,2},{4,5},{5,4},{6,7},{7,6},{8,9},{9,8},{10,11... | collective-permute-start | bytes 393224 | tf_op jit(solution)/shard_map/ppermute | solution.py:122
  32.7 2.5 %collective-permute-done.12.refs_2_ = bf16[32,1024]{1,0:T(8,128)(2,1)S(1)} collective-permute-done((bf16[32,1024]{1,0:T(8,128)(2,1)S(1)}, bf16[32,1024]{1,0:T(8,128)(2,1)S(1)}, u32[]{:S(2)}, u32[]{:S(2)}) %collective-permute-start.12) | collective-permute-done | bytes 65568 | tf_op jit(solution)/shard_map/ppermute | solution.py:122
  35.3 0.7 %add.3 = f32[32,1024]{1,0:T(8,128)} add(f32[32,1024]{1,0:T(8,128)S(1)} %shard_map.43, f32[32,1024]{1,0:T(8,128)S(1)} %collective-permute-done.13) | non-fusion elementwise | flops 32768 | bytes 393216 | tf_op jit(solution)/shard_map/add | solution.py:159
  (16 shorter events, 0.2 us)
Async XLA Ops:
  0.0 1.4 %collective-permute-start = (bf16[32,512]{1,0:T(8,128)(2,1)}, bf16[32,512]{1,0:T(8,128)(2,1)S(1)}, u32[]{:S(2)}, u32[]{:S(2)}) collective-permute-start(bf16[32,512]{1,0:T(8,128)(2,1)} %param.3), channel_id=1, source_target_pairs={{0,1},{1,0},{2,3},{3,2},{4,5},{5,4},{6,7},{7,6},{8,9},{9,8},{10,11... | collective-permute-start | bytes 98312 | tf_op jit(solution)/shard_map/ppermute | solution.py:122
  2.2 8.7 %collective-permute-start.1 = (bf16[64,512]{1,0:T(8,128)(2,1)S(1)}, bf16[64,512]{1,0:T(8,128)(2,1)S(1)}, u32[]{:S(2)}, u32[]{:S(2)}) collective-permute-start(bf16[64,512]{1,0:T(8,128)(2,1)S(1)} %pad_maximum_fusion), channel_id=1, source_target_pairs={{0,12},{1,9},{2,14},{3,11},{4,8},{5,13},{6,10},{7,15},{8,4},{9,1},... | collective-permute-start | bytes 196616 | tf_op jit(solution)/shard_map/ppermute | solution.py:122
  5.6 5.2 %collective-permute-start.2 = (bf16[64,512]{1,0:T(8,128)(2,1)S(1)}, bf16[64,512]{1,0:T(8,128)(2,1)S(1)}, u32[]{:S(2)}, u32[]{:S(2)}) collective-permute-start(bf16[64,512]{1,0:T(8,128)(2,1)S(1)} %pad_maximum_fusion), channel_id=1, source_target_pairs={{0,0},{1,5},{2,2},{3,7},{4,4},{5,1},{6,6},{7,3},{8,8},{9,13},{10,1... | collective-permute-start | bytes 196616 | tf_op jit(solution)/shard_map/ppermute | solution.py:122
  10.9 4.8 %collective-permute-start.5 = (bf16[128,512]{1,0:T(8,128)(2,1)S(1)}, bf16[128,512]{1,0:T(8,128)(2,1)S(1)}, u32[]{:S(2)}, u32[]{:S(2)}) collective-permute-start(bf16[128,512]{1,0:T(8,128)(2,1)S(1)} %constant_dynamic-update-slice_fusion.rows), channel_id=1, source_target_pairs={{0,2},{1,3},{2,0},{3,1},{4,6},{5,7},{6,4},{7,5},{8,10},{9,11},{10,... | collective-permute-start | bytes 393224 | tf_op jit(solution)/shard_map/ppermute | solution.py:122
  12.8 3.5 %collective-permute-start.4 = (bf16[128,1024]{1,0:T(8,128)(2,1)S(1)}, bf16[128,1024]{1,0:T(8,128)(2,1)S(1)}, u32[]{:S(2)}, u32[]{:S(2)}) collective-permute-start(bf16[128,1024]{1,0:T(8,128)(2,1)S(1)} %shard_map.38), channel_id=1, source_target_pairs={{0,1},{1,0},{2,3},{3,2},{4,5},{5,4},{6,7},{7,6},{8,9},{9,8},{10,11... | collective-permute-start | bytes 786440 | tf_op jit(solution)/shard_map/ppermute | solution.py:122
  16.4 5.9 %collective-permute-start.9 = (bf16[128,1024]{1,0:T(8,128)(2,1)S(1)}, bf16[128,1024]{1,0:T(8,128)(2,1)S(1)}, u32[]{:S(2)}, u32[]{:S(2)}) collective-permute-start(bf16[128,1024]{1,0:T(8,128)(2,1)S(1)} %shard_map.39), channel_id=1, source_target_pairs={{0,1},{1,0},{2,3},{3,2},{4,5},{5,4},{6,7},{7,6},{8,9},{9,8},{10,11... | collective-permute-start | bytes 786440 | tf_op jit(solution)/shard_map/ppermute | solution.py:122
  16.8 1.4 %collective-permute-start.3 = (bf16[128,512]{1,0:T(8,128)(2,1)S(1)}, bf16[128,512]{1,0:T(8,128)(2,1)S(1)}, u32[]{:S(2)}, u32[]{:S(2)}) collective-permute-start(bf16[128,512]{1,0:T(8,128)(2,1)S(1)} %constant_dynamic-update-slice_fusion.rows), channel_id=1, source_target_pairs={{0,1},{1,0},{2,3},{3,2},{4,5},{5,4},{6,7},{7,6},{8,9},{9,8},{10,11... | collective-permute-start | bytes 393224 | tf_op jit(solution)/shard_map/ppermute | solution.py:122
  16.9 5.3 %collective-permute-start.8 = (bf16[128,512]{1,0:T(8,128)(2,1)S(1)}, bf16[128,512]{1,0:T(8,128)(2,1)S(1)}, u32[]{:S(2)}, u32[]{:S(2)}) collective-permute-start(bf16[128,512]{1,0:T(8,128)(2,1)S(1)} %collective-permute-done.5.rows), channel_id=1, source_target_pairs={{0,1},{1,0},{2,3},{3,2},{4,5},{5,4},{6,7},{7,6},{8,9},{9,8},{10,11... | collective-permute-start | bytes 393224 | tf_op jit(solution)/shard_map/ppermute | solution.py:122
  18.7 12.5 %collective-permute-start.6 = (bf16[64,1024]{1,0:T(8,128)(2,1)S(1)}, bf16[64,1024]{1,0:T(8,128)(2,1)S(1)}, u32[]{:S(2)}, u32[]{:S(2)}) collective-permute-start(bf16[64,1024]{1,0:T(8,128)(2,1)S(1)} %get-tuple-element.29), channel_id=1, source_target_pairs={{0,8},{1,13},{2,10},{3,15},{4,12},{5,9},{6,14},{7,11},{8,0},{9,5},... | collective-permute-start | bytes 393224 | tf_op jit(solution)/shard_map/ppermute | solution.py:122
  21.6 9.7 %collective-permute-start.7 = (bf16[64,1024]{1,0:T(8,128)(2,1)S(1)}, bf16[64,1024]{1,0:T(8,128)(2,1)S(1)}, u32[]{:S(2)}, u32[]{:S(2)}) collective-permute-start(bf16[64,1024]{1,0:T(8,128)(2,1)S(1)} %get-tuple-element.30), channel_id=1, source_target_pairs={{0,4},{1,1},{2,6},{3,3},{4,0},{5,5},{6,2},{7,7},{8,12},{9,9},{10,1... | collective-permute-start | bytes 393224 | tf_op jit(solution)/shard_map/ppermute | solution.py:122
  22.9 8.4 %collective-permute-start.10 = (bf16[64,1024]{1,0:T(8,128)(2,1)S(1)}, bf16[64,1024]{1,0:T(8,128)(2,1)S(1)}, u32[]{:S(2)}, u32[]{:S(2)}) collective-permute-start(bf16[64,1024]{1,0:T(8,128)(2,1)S(1)} %get-tuple-element.32), channel_id=1, source_target_pairs={{0,6},{1,3},{2,4},{3,1},{4,2},{5,7},{6,0},{7,5},{8,14},{9,11},{10,... | collective-permute-start | bytes 393224 | tf_op jit(solution)/shard_map/ppermute | solution.py:122
  24.2 8.5 %collective-permute-start.11 = (bf16[32,1024]{1,0:T(8,128)(2,1)S(1)}, bf16[32,1024]{1,0:T(8,128)(2,1)S(1)}, u32[]{:S(2)}, u32[]{:S(2)}) collective-permute-start(bf16[32,1024]{1,0:T(8,128)(2,1)S(1)} %get-tuple-element.33), channel_id=1, source_target_pairs={{0,10},{1,15},{2,8},{3,13},{4,14},{5,11},{6,12},{7,9},{8,2},{9,7},... | collective-permute-start | bytes 196616 | tf_op jit(solution)/shard_map/ppermute | solution.py:122
  24.6 10.6 %collective-permute-start.12 = (bf16[32,1024]{1,0:T(8,128)(2,1)S(1)}, bf16[32,1024]{1,0:T(8,128)(2,1)S(1)}, u32[]{:S(2)}, u32[]{:S(2)}) collective-permute-start(bf16[32,1024]{1,0:T(8,128)(2,1)S(1)} %get-tuple-element.34), channel_id=1, source_target_pairs={{0,11},{1,14},{2,9},{3,12},{4,15},{5,10},{6,13},{7,8},{8,3},{9,6},... | collective-permute-start | bytes 196616 | tf_op jit(solution)/shard_map/ppermute | solution.py:122
  31.4 3.9 %collective-permute-start.13 = (f32[32,1024]{1,0:T(8,128)S(1)}, f32[32,1024]{1,0:T(8,128)S(1)}, u32[]{:S(2)}, u32[]{:S(2)}) collective-permute-start(f32[32,1024]{1,0:T(8,128)S(1)} %get-tuple-element.35), channel_id=1, source_target_pairs={{0,1},{1,0},{2,3},{3,2},{4,5},{5,4},{6,7},{7,6},{8,9},{9,8},{10,11... | collective-permute-start | bytes 393224 | tf_op jit(solution)/shard_map/ppermute | solution.py:122

commit v3 on v2

--- a/solution.py
+++ b/solution.py
@@ -6,7 +6,6 @@
 from jax.sharding import PartitionSpec as P
 
 AXES = ("lm", "env")
-HEAVY = 10**11
 VMEM = pl.BlockSpec(memory_space=pltpu.VMEM)
 PARAMS = pltpu.CompilerParams(vmem_limit_bytes=16 * 2**20)
 
@@ -68,27 +67,6 @@
         at += out.shape[0]
 
 
-def add_body(*refs):
-    *parts, out = refs
-    total = parts[0][...].astype(jnp.float32)
-    for part in parts[1:]:
-        total += part[...].astype(jnp.float32)
-    out[...] = total
-
-
-def add(*parts, weight=1):
-    return pl.pallas_call(
-        add_body,
-        out_shape=jax.ShapeDtypeStruct(parts[0].shape, jnp.float32),
-        in_specs=[VMEM] * len(parts),
-        out_specs=VMEM,
-        compiler_params=PARAMS,
-        cost_estimate=pl.CostEstimate(
-            flops=weight * HEAVY, bytes_accessed=0, transcendentals=0
-        ),
-    )(*parts)
-
-
 def call(body, sizes, *args, rounds=1):
     rows, landmarks, _, weights = args[:4]
     read = sum(arg.size * arg.dtype.itemsize for arg in args)
@@ -127,15 +105,21 @@
     def local(env_desc, landmarks, whitening):
         rows = env_desc.shape[0]
 
-        chip_rows = jnp.concatenate([env_desc, swap(env_desc)])
-        landmarks, chip_rows = lax.optimization_barrier((landmarks, chip_rows))
+        peer = swap(env_desc)
+        landmarks, peer = lax.optimization_barrier((landmarks, peer))
+        chip_rows = jnp.concatenate([env_desc, peer])
         got = [exchange(chip_rows, (a * inner, b * inner)) for a, b in reversed(list(zip(*steps)))]
         landmarks, whitening, land_sq = load(landmarks, whitening)
-        got, land_sq = lax.optimization_barrier((got, land_sq))
-        got = jnp.concatenate(got[::-1])
-        lines = [got] + [exchange(got, (k, k)) for k in range(1, inner)]
+        got = got[::-1]
+        lines = [got]
+        for k in range(1, inner):
+            line = [exchange(block, (k, k)) for block in got]
+            lines.append(line)
+        lines = [jnp.concatenate(line) for line in lines]
 
         tables = (landmarks, land_sq, whitening)
+        seconds = [swap(lines[0])]
+        seconds[0], *lines[1:] = lax.optimization_barrier(seconds + lines[1:])
         given = [
             call(give_body, [first.shape[0]], first, *tables, rounds=20 if k else 1)[0]
             for k, first in enumerate(lines)
@@ -143,20 +127,16 @@
         taken = [swap(given[0])]
         taken[0], *given[1:] = lax.optimization_barrier(taken + given[1:])
         taken += [swap(block) for block in given[1:]]
-        parts = []
+        seconds += [swap(first) for first in lines[1:]]
+        near, far = [], []
         for k, first in enumerate(lines):
             sizes = [2 * rows] * (outer // 2)
-            if k == inner - 1:
-                sizes[-1:] = [rows, rows]
-            blocks = call(keep_body, sizes, swap(first), *tables, taken[k])
+            blocks = call(keep_body, sizes, seconds[k], *tables, taken[k])
             for i in reversed(range(outer // 2)):
                 by = (steps[1][i] * inner + k, steps[0][i] * inner + k)
-                if k == inner - 1 and i == outer // 2 - 1:
-                    last = [exchange(blocks[-1], by), exchange(blocks[-2], by, 1)]
-                else:
-                    parts.append(exchange(blocks[i], by))
-        total = add(*parts)
-        return add(total[rows:], *last) + swap(total[:rows])
+                (far if i else near).append(exchange(blocks[i], by))
+        total = sum(part.astype(jnp.float32) for part in far + near)
+        return total[rows:] + swap(total[:rows])
 
     return jax.shard_map(
         local,

time: 36.2 us -> 34.3 us (0.948)
  the two profiles are of different devices: /device:TPU:1 before, /device:TPU:0 now
where the time goes in v3:
time: 34.3 us; the launch traced here: 34.1 us
  starting transfers between devices  17.6 us (51%)
  waiting for transfers between devices  10.4 us (30%)
  Pallas kernels  4.35 us (13%)
  local copies, waits for them, and re-layouts  0.78 us (2%)
  other arithmetic  0.75 us (2%)
    ppermute x14, starting transfers between devices, exchange(): return lax.ppermute(block, AXES, pairs)  17.6 us
    ppermute x14, waiting for transfers between devices, exchange(): return lax.ppermute(block, AXES, pairs)  10.4 us
    pallas_call x4, Pallas kernels, call(): pl.pallas_call(body, out_shape=[jax.ShapeDtypeStruct((size, weights.shape...  2.34 us
    pallas_call x1, Pallas kernels, load(): pl.pallas_call(load_body, out_shape=[jax.ShapeDtypeStruct(landmarks.shape...  2 us
    unnamed x2, local copies, waits for them, and re-layouts  0.77 us
  transfers between devices with their start and end apart: 14, of which 5 were waited for; matrix products, arithmetic and copies ran while one was open for 2% of the time, Pallas kernels for 13%

profile of v3, /device:TPU:0, one launch (start us, length us, event | category | flops | bytes accessed | tf_op | source)
XLA Modules:
  0.0 34.1 jit_solution(14182387906223708083)
XLA Ops:
  0.0 0.5 %collective-permute-start = (bf16[32,512]{1,0:T(8,128)(2,1)}, bf16[32,512]{1,0:T(8,128)(2,1)S(1)}, u32[]{:S(2)}, u32[]{:S(2)}) collective-permute-start(bf16[32,512]{1,0:T(8,128)(2,1)} %param.3), channel_id=1, source_target_pairs={{0,1},{1,0},{2,3},{3,2},{4,5},{5,4},{6,7},{7,6},{8,9},{9,8},{10,11... | collective-permute-start | bytes 98312 | tf_op jit(solution)/shard_map/ppermute | solution.py:100
  0.5 0.8 %constant_dynamic-update-slice_fusion.1 = bf16[64,512]{1,0:T(8,128)(2,1)S(1)} fusion(bf16[32,512]{1,0:T(8,128)(2,1)} %param.3), kind=kLoop, calls=%fused_computation.4 | loop fusion | bytes 65536
  1.2 0.3 collective-permute-done
  1.5 4.9 %collective-permute-start.2 = (bf16[64,512]{1,0:T(8,128)(2,1)S(1)}, bf16[64,512]{1,0:T(8,128)(2,1)S(1)}, u32[]{:S(2)}, u32[]{:S(2)}) collective-permute-start(bf16[64,512]{1,0:T(8,128)(2,1)S(1)} %constant_dynamic-update-slice_fusion), channel_id=1, source_target_pairs={{0,12},{1,9},{2,14},{3,11},{4,8},{5,13},{6,10},{7,15},{8,4},{9,1},... | collective-permute-start | bytes 196616 | tf_op jit(solution)/shard_map/ppermute | solution.py:100
  6.5 0.7 %collective-permute-start.1 = (bf16[64,512]{1,0:T(8,128)(2,1)S(1)}, bf16[64,512]{1,0:T(8,128)(2,1)S(1)}, u32[]{:S(2)}, u32[]{:S(2)}) collective-permute-start(bf16[64,512]{1,0:T(8,128)(2,1)S(1)} %constant_dynamic-update-slice_fusion), channel_id=1, source_target_pairs={{0,0},{1,5},{2,2},{3,7},{4,4},{5,1},{6,6},{7,3},{8,8},{9,13},{10,1... | collective-permute-start | bytes 196616 | tf_op jit(solution)/shard_map/ppermute | solution.py:100
  7.1 2.0 %shard_map.37 = (bf16[512,512]{1,0:T(8,128)(2,1)S(1)}, bf16[512,1024]{1,0:T(8,128)(2,1)S(1)}, f32[8,512]{1,0:T(8,128)S(1)}) custom-call(bf16[512,512]{1,0:T(8,128)(2,1)} %landmarks, bf16[512,1024]{1,0:T(8,128)(2,1)} %weights.1), custom_call_target="tpu_custom_call" | custom-call | flops 1000000000 | tf_op jit(solution)/shard_map/pallas_call | solution.py:31
  9.2 1.6 %collective-permute-start.4 = (bf16[64,512]{1,0:T(8,128)(2,1)S(1)}, bf16[64,512]{1,0:T(8,128)(2,1)S(1)}, u32[]{:S(2)}, u32[]{:S(2)}) collective-permute-start(bf16[64,512]{1,0:T(8,128)(2,1)S(1)} %collective-permute-done.1), channel_id=1, source_target_pairs={{0,2},{1,3},{2,0},{3,1},{4,6},{5,7},{6,4},{7,5},{8,10},{9,11},{10,... | collective-permute-start | bytes 196616 | tf_op jit(solution)/shard_map/ppermute | solution.py:100
  10.8 0.6 %collective-permute-start.5 = (bf16[64,512]{1,0:T(8,128)(2,1)S(1)}, bf16[64,512]{1,0:T(8,128)(2,1)S(1)}, u32[]{:S(2)}, u32[]{:S(2)}) collective-permute-start(bf16[64,512]{1,0:T(8,128)(2,1)S(1)} %collective-permute-done.2), channel_id=1, source_target_pairs={{0,2},{1,3},{2,0},{3,1},{4,6},{5,7},{6,4},{7,5},{8,10},{9,11},{10,... | collective-permute-start | bytes 196616 | tf_op jit(solution)/shard_map/ppermute | solution.py:100
  11.3 0.8 %collective-permute-start.3 = (bf16[128,512]{1,0:T(8,128)(2,1)S(1)}, bf16[128,512]{1,0:T(8,128)(2,1)S(1)}, u32[]{:S(2)}, u32[]{:S(2)}) collective-permute-start(bf16[128,512]{1,0:T(8,128)(2,1)S(1)} %constant_dynamic-update-slice_fusion.2.rows), channel_id=1, source_target_pairs={{0,1},{1,0},{2,3},{3,2},{4,5},{5,4},{6,7},{7,6},{8,9},{9,8},{10,11... | collective-permute-start | bytes 393224 | tf_op jit(solution)/shard_map/ppermute | solution.py:100
  12.2 0.6 %shard_map.38 = bf16[128,1024]{1,0:T(8,128)(2,1)S(1)} custom-call(bf16[128,512]{1,0:T(8,128)(2,1)S(1)} %constant_dynamic-update-slice_fusion.2.rows, bf16[512,512]{1,0:T(8,128)(2,1)S(1)} %get-tuple-element.21.landmarks, f32[8,512]{1,0:T(8,128)S(1)} %get-tuple-element.22.land_sq, bf16[512,1024]{1,0:T(8,128)(2,1)S(1)} %get-tuple-element.23.weights), custom_call_target="tpu_custom_call" | custom-call | flops 201326592 | bytes 1720320 | tf_op jit(solution)/shard_map/pallas_call | solution.py:78
  12.8 0.1 collective-permute-start.6
  12.8 2.8 %collective-permute-done.5 = bf16[64,512]{1,0:T(8,128)(2,1)S(1)} collective-permute-done((bf16[64,512]{1,0:T(8,128)(2,1)S(1)}, bf16[64,512]{1,0:T(8,128)(2,1)S(1)}, u32[]{:S(2)}, u32[]{:S(2)}) %collective-permute-start.5) | collective-permute-done | bytes 65568 | tf_op jit(solution)/shard_map/ppermute | solution.py:100
  15.6 0.6 %shard_map.39 = bf16[128,1024]{1,0:T(8,128)(2,1)S(1)} custom-call(bf16[128,512]{1,0:T(8,128)(2,1)S(1)} %pad_maximum_fusion.rows, bf16[512,512]{1,0:T(8,128)(2,1)S(1)} %get-tuple-element.21.landmarks, f32[8,512]{1,0:T(8,128)S(1)} %get-tuple-element.22.land_sq, bf16[512,1024]{1,0:T(8,128)(2,1)S(1)} %get-tuple-element.23.weights), custom_call_target="tpu_custom_call" | custom-call | flops 4026531840 | bytes 34406400 | tf_op jit(solution)/shard_map/pallas_call | solution.py:78
  16.3 0.2 collective-permute-start.9
  16.4 0.4 %collective-permute-start.8 = (bf16[128,512]{1,0:T(8,128)(2,1)S(1)}, bf16[128,512]{1,0:T(8,128)(2,1)S(1)}, u32[]{:S(2)}, u32[]{:S(2)}) collective-permute-start(bf16[128,512]{1,0:T(8,128)(2,1)S(1)} %pad_maximum_fusion.rows), channel_id=1, source_target_pairs={{0,1},{1,0},{2,3},{3,2},{4,5},{5,4},{6,7},{7,6},{8,9},{9,8},{10,11... | collective-permute-start | bytes 393224 | tf_op jit(solution)/shard_map/ppermute | solution.py:100
  16.8 0.6 %shard_map.40 = (bf16[64,1024]{1,0:T(8,128)(2,1)S(1)}, bf16[64,1024]{1,0:T(8,128)(2,1)S(1)}) custom-call(bf16[128,512]{1,0:T(8,128)(2,1)S(1)} %collective-permute-done.3.rows, bf16[512,512]{1,0:T(8,128)(2,1)S(1)} %get-tuple-element.21.landmarks, f32[8,512]{1,0:T(8,128)S(1)} %get-tuple-element.22.land_sq, bf16[512,1024]{1,0:T(8,128)(2,1)S(1)} %get-tuple-element.23.weights, ...), custom_call_target="tpu_custom_call" | custom-call | flops 201326592 | bytes 1982464 | tf_op jit(solution)/shard_map/pallas_call | solution.py:78
  17.5 4.1 %collective-permute-start.11 = (bf16[64,1024]{1,0:T(8,128)(2,1)S(1)}, bf16[64,1024]{1,0:T(8,128)(2,1)S(1)}, u32[]{:S(2)}, u32[]{:S(2)}) collective-permute-start(bf16[64,1024]{1,0:T(8,128)(2,1)S(1)} %get-tuple-element.29), channel_id=1, source_target_pairs={{0,4},{1,1},{2,6},{3,3},{4,0},{5,5},{6,2},{7,7},{8,12},{9,9},{10,1... | collective-permute-start | bytes 393224 | tf_op jit(solution)/shard_map/ppermute | solution.py:100
  21.7 0.6 %shard_map.41 = (bf16[64,1024]{1,0:T(8,128)(2,1)S(1)}, bf16[64,1024]{1,0:T(8,128)(2,1)S(1)}) custom-call(bf16[128,512]{1,0:T(8,128)(2,1)S(1)} %collective-permute-done.8.rows, bf16[512,512]{1,0:T(8,128)(2,1)S(1)} %get-tuple-element.21.landmarks, f32[8,512]{1,0:T(8,128)S(1)} %get-tuple-element.22.land_sq, bf16[512,1024]{1,0:T(8,128)(2,1)S(1)} %get-tuple-element.23.weights, ...), custom_call_target="tpu_custom_call" | custom-call | flops 201326592 | bytes 1982464 | tf_op jit(solution)/shard_map/pallas_call | solution.py:78
  22.3 1.4 %collective-permute-start.10 = (bf16[64,1024]{1,0:T(8,128)(2,1)S(1)}, bf16[64,1024]{1,0:T(8,128)(2,1)S(1)}, u32[]{:S(2)}, u32[]{:S(2)}) collective-permute-start(bf16[64,1024]{1,0:T(8,128)(2,1)S(1)} %get-tuple-element.28), channel_id=1, source_target_pairs={{0,10},{1,15},{2,8},{3,13},{4,14},{5,11},{6,12},{7,9},{8,2},{9,7},... | collective-permute-start | bytes 393224 | tf_op jit(solution)/shard_map/ppermute | solution.py:100
  23.6 2.3 %collective-permute-start.12 = (bf16[64,1024]{1,0:T(8,128)(2,1)S(1)}, bf16[64,1024]{1,0:T(8,128)(2,1)S(1)}, u32[]{:S(2)}, u32[]{:S(2)}) collective-permute-start(bf16[64,1024]{1,0:T(8,128)(2,1)S(1)} %get-tuple-element.30), channel_id=1, source_target_pairs={{0,6},{1,3},{2,4},{3,1},{4,2},{5,7},{6,0},{7,5},{8,14},{9,11},{10,... | collective-permute-start | bytes 393224 | tf_op jit(solution)/shard_map/ppermute | solution.py:100
  25.9 4.1 %collective-permute-done.7 = bf16[64,1024]{1,0:T(8,128)(2,1)S(1)} collective-permute-done((bf16[64,1024]{1,0:T(8,128)(2,1)S(1)}, bf16[64,1024]{1,0:T(8,128)(2,1)S(1)}, u32[]{:S(2)}, u32[]{:S(2)}) %collective-permute-start.7) | collective-permute-done | bytes 131104 | tf_op jit(solution)/shard_map/ppermute | solution.py:100
  30.1 1.8 %collective-permute-done.10 = bf16[64,1024]{1,0:T(8,128)(2,1)S(1)} collective-permute-done((bf16[64,1024]{1,0:T(8,128)(2,1)S(1)}, bf16[64,1024]{1,0:T(8,128)(2,1)S(1)}, u32[]{:S(2)}, u32[]{:S(2)}) %collective-permute-start.10) | collective-permute-done | bytes 131104 | tf_op jit(solution)/shard_map/ppermute | solution.py:100
  32.1 1.3 %collective-permute-done.13 = f32[32,1024]{1,0:T(8,128)S(1)} collective-permute-done((f32[32,1024]{1,0:T(8,128)S(1)}, f32[32,1024]{1,0:T(8,128)S(1)}, u32[]{:S(2)}, u32[]{:S(2)}) %collective-permute-start.13) | collective-permute-done | bytes 131104 | tf_op jit(solution)/shard_map/ppermute | solution.py:100
  33.4 0.7 %slice_add_fusion = f32[32,1024]{1,0:T(8,128)} fusion(f32[32,1024]{1,0:T(8,128)S(1)} %collective-permute-done.13, f32[64,1024]{1,0:T(8,128)S(1)} %convert_add_fusion), kind=kLoop, calls=%fused_computation.1 | loop fusion | flops 32768 | bytes 393216 | tf_op jit(solution)/shard_map/add | solution.py:139
  (17 shorter events, 0.3 us)
Async XLA Ops:
  0.0 1.5 %collective-permute-start = (bf16[32,512]{1,0:T(8,128)(2,1)}, bf16[32,512]{1,0:T(8,128)(2,1)S(1)}, u32[]{:S(2)}, u32[]{:S(2)}) collective-permute-start(bf16[32,512]{1,0:T(8,128)(2,1)} %param.3), channel_id=1, source_target_pairs={{0,1},{1,0},{2,3},{3,2},{4,5},{5,4},{6,7},{7,6},{8,9},{9,8},{10,11... | collective-permute-start | bytes 98312 | tf_op jit(solution)/shard_map/ppermute | solution.py:100
  1.5 9.2 %collective-permute-start.2 = (bf16[64,512]{1,0:T(8,128)(2,1)S(1)}, bf16[64,512]{1,0:T(8,128)(2,1)S(1)}, u32[]{:S(2)}, u32[]{:S(2)}) collective-permute-start(bf16[64,512]{1,0:T(8,128)(2,1)S(1)} %constant_dynamic-update-slice_fusion), channel_id=1, source_target_pairs={{0,12},{1,9},{2,14},{3,11},{4,8},{5,13},{6,10},{7,15},{8,4},{9,1},... | collective-permute-start | bytes 196616 | tf_op jit(solution)/shard_map/ppermute | solution.py:100
  6.5 2.7 %collective-permute-start.1 = (bf16[64,512]{1,0:T(8,128)(2,1)S(1)}, bf16[64,512]{1,0:T(8,128)(2,1)S(1)}, u32[]{:S(2)}, u32[]{:S(2)}) collective-permute-start(bf16[64,512]{1,0:T(8,128)(2,1)S(1)} %constant_dynamic-update-slice_fusion), channel_id=1, source_target_pairs={{0,0},{1,5},{2,2},{3,7},{4,4},{5,1},{6,6},{7,3},{8,8},{9,13},{10,1... | collective-permute-start | bytes 196616 | tf_op jit(solution)/shard_map/ppermute | solution.py:100
  9.2 6.5 %collective-permute-start.4 = (bf16[64,512]{1,0:T(8,128)(2,1)S(1)}, bf16[64,512]{1,0:T(8,128)(2,1)S(1)}, u32[]{:S(2)}, u32[]{:S(2)}) collective-permute-start(bf16[64,512]{1,0:T(8,128)(2,1)S(1)} %collective-permute-done.1), channel_id=1, source_target_pairs={{0,2},{1,3},{2,0},{3,1},{4,6},{5,7},{6,4},{7,5},{8,10},{9,11},{10,... | collective-permute-start | bytes 196616 | tf_op jit(solution)/shard_map/ppermute | solution.py:100
  10.8 4.9 %collective-permute-start.5 = (bf16[64,512]{1,0:T(8,128)(2,1)S(1)}, bf16[64,512]{1,0:T(8,128)(2,1)S(1)}, u32[]{:S(2)}, u32[]{:S(2)}) collective-permute-start(bf16[64,512]{1,0:T(8,128)(2,1)S(1)} %collective-permute-done.2), channel_id=1, source_target_pairs={{0,2},{1,3},{2,0},{3,1},{4,6},{5,7},{6,4},{7,5},{8,10},{9,11},{10,... | collective-permute-start | bytes 196616 | tf_op jit(solution)/shard_map/ppermute | solution.py:100
  11.3 4.3 %collective-permute-start.3 = (bf16[128,512]{1,0:T(8,128)(2,1)S(1)}, bf16[128,512]{1,0:T(8,128)(2,1)S(1)}, u32[]{:S(2)}, u32[]{:S(2)}) collective-permute-start(bf16[128,512]{1,0:T(8,128)(2,1)S(1)} %constant_dynamic-update-slice_fusion.2.rows), channel_id=1, source_target_pairs={{0,1},{1,0},{2,3},{3,2},{4,5},{5,4},{6,7},{7,6},{8,9},{9,8},{10,11... | collective-permute-start | bytes 393224 | tf_op jit(solution)/shard_map/ppermute | solution.py:100
  12.8 3.5 %collective-permute-start.6 = (bf16[128,1024]{1,0:T(8,128)(2,1)S(1)}, bf16[128,1024]{1,0:T(8,128)(2,1)S(1)}, u32[]{:S(2)}, u32[]{:S(2)}) collective-permute-start(bf16[128,1024]{1,0:T(8,128)(2,1)S(1)} %shard_map.38), channel_id=1, source_target_pairs={{0,1},{1,0},{2,3},{3,2},{4,5},{5,4},{6,7},{7,6},{8,9},{9,8},{10,11... | collective-permute-start | bytes 786440 | tf_op jit(solution)/shard_map/ppermute | solution.py:100
  16.3 5.4 %collective-permute-start.9 = (bf16[128,1024]{1,0:T(8,128)(2,1)S(1)}, bf16[128,1024]{1,0:T(8,128)(2,1)S(1)}, u32[]{:S(2)}, u32[]{:S(2)}) collective-permute-start(bf16[128,1024]{1,0:T(8,128)(2,1)S(1)} %shard_map.39), channel_id=1, source_target_pairs={{0,1},{1,0},{2,3},{3,2},{4,5},{5,4},{6,7},{7,6},{8,9},{9,8},{10,11... | collective-permute-start | bytes 786440 | tf_op jit(solution)/shard_map/ppermute | solution.py:100
  16.4 5.2 %collective-permute-start.8 = (bf16[128,512]{1,0:T(8,128)(2,1)S(1)}, bf16[128,512]{1,0:T(8,128)(2,1)S(1)}, u32[]{:S(2)}, u32[]{:S(2)}) collective-permute-start(bf16[128,512]{1,0:T(8,128)(2,1)S(1)} %pad_maximum_fusion.rows), channel_id=1, source_target_pairs={{0,1},{1,0},{2,3},{3,2},{4,5},{5,4},{6,7},{7,6},{8,9},{9,8},{10,11... | collective-permute-start | bytes 393224 | tf_op jit(solution)/shard_map/ppermute | solution.py:100
  17.4 12.6 %collective-permute-start.7 = (bf16[64,1024]{1,0:T(8,128)(2,1)S(1)}, bf16[64,1024]{1,0:T(8,128)(2,1)S(1)}, u32[]{:S(2)}, u32[]{:S(2)}) collective-permute-start(bf16[64,1024]{1,0:T(8,128)(2,1)S(1)} %get-tuple-element.26), channel_id=1, source_target_pairs={{0,8},{1,13},{2,10},{3,15},{4,12},{5,9},{6,14},{7,11},{8,0},{9,5},... | collective-permute-start | bytes 393224 | tf_op jit(solution)/shard_map/ppermute | solution.py:100
  17.5 12.6 %collective-permute-start.11 = (bf16[64,1024]{1,0:T(8,128)(2,1)S(1)}, bf16[64,1024]{1,0:T(8,128)(2,1)S(1)}, u32[]{:S(2)}, u32[]{:S(2)}) collective-permute-start(bf16[64,1024]{1,0:T(8,128)(2,1)S(1)} %get-tuple-element.29), channel_id=1, source_target_pairs={{0,4},{1,1},{2,6},{3,3},{4,0},{5,5},{6,2},{7,7},{8,12},{9,9},{10,1... | collective-permute-start | bytes 393224 | tf_op jit(solution)/shard_map/ppermute | solution.py:100
  22.3 9.6 %collective-permute-start.10 = (bf16[64,1024]{1,0:T(8,128)(2,1)S(1)}, bf16[64,1024]{1,0:T(8,128)(2,1)S(1)}, u32[]{:S(2)}, u32[]{:S(2)}) collective-permute-start(bf16[64,1024]{1,0:T(8,128)(2,1)S(1)} %get-tuple-element.28), channel_id=1, source_target_pairs={{0,10},{1,15},{2,8},{3,13},{4,14},{5,11},{6,12},{7,9},{8,2},{9,7},... | collective-permute-start | bytes 393224 | tf_op jit(solution)/shard_map/ppermute | solution.py:100
  23.6 8.3 %collective-permute-start.12 = (bf16[64,1024]{1,0:T(8,128)(2,1)S(1)}, bf16[64,1024]{1,0:T(8,128)(2,1)S(1)}, u32[]{:S(2)}, u32[]{:S(2)}) collective-permute-start(bf16[64,1024]{1,0:T(8,128)(2,1)S(1)} %get-tuple-element.30), channel_id=1, source_target_pairs={{0,6},{1,3},{2,4},{3,1},{4,2},{5,7},{6,0},{7,5},{8,14},{9,11},{10,... | collective-permute-start | bytes 393224 | tf_op jit(solution)/shard_map/ppermute | solution.py:100
  32.0 1.4 %collective-permute-start.13 = (f32[32,1024]{1,0:T(8,128)S(1)}, f32[32,1024]{1,0:T(8,128)S(1)}, u32[]{:S(2)}, u32[]{:S(2)}) collective-permute-start(f32[32,1024]{1,0:T(8,128)S(1)} %slice.9), channel_id=1, source_target_pairs={{0,1},{1,0},{2,3},{3,2},{4,5},{5,4},{6,7},{7,6},{8,9},{9,8},{10,11... | collective-permute-start | bytes 393224 | tf_op jit(solution)/shard_map/ppermute | solution.py:100

commit v4 on v3

--- a/solution.py
+++ b/solution.py
@@ -1,3 +1,5 @@
+import functools
+
 import jax
 import jax.numpy as jnp
 from jax import lax
@@ -6,6 +8,7 @@
 from jax.sharding import PartitionSpec as P
 
 AXES = ("lm", "env")
+HEAVY = 5*10**9
 VMEM = pl.BlockSpec(memory_space=pltpu.VMEM)
 PARAMS = pltpu.CompilerParams(vmem_limit_bytes=16 * 2**20)
 
@@ -53,36 +56,69 @@
     return jnp.dot(kern, weights, preferred_element_type=jnp.float32)
 
 
-def give_body(rows, landmarks, land_sq, weights, out):
+def sums_body(rows, landmarks, land_sq, weights, out):
     sums = kernel_sums(rows[...], landmarks[...], land_sq[0:1], weights[...])
     out[...] = sums.astype(out.dtype)
 
 
-def keep_body(rows, landmarks, land_sq, weights, taken, *outs):
-    sums = kernel_sums(rows[...], landmarks[...], land_sq[0:1], weights[...])
-    sums += taken[...].astype(jnp.float32)
+def line_part(dtype, weight, rows, landmarks, land_sq, weights):
+    args = (rows, landmarks, land_sq, weights)
+    count, depth, width = rows.shape[0], landmarks.shape[0], weights.shape[1]
+    return pl.pallas_call(
+        sums_body,
+        out_shape=jax.ShapeDtypeStruct((count, width), dtype),
+        in_specs=[VMEM] * 4,
+        out_specs=VMEM,
+        compiler_params=PARAMS,
+        cost_estimate=pl.CostEstimate(
+            flops=weight * 2 * count * depth * (rows.shape[1] + width),
+            bytes_accessed=sum(arg.size * arg.dtype.itemsize for arg in args),
+            transcendentals=count * depth,
+        ),
+    )(*args)
+
+
+def join_body(kept, taken, *outs):
     at = 0
     for out in outs:
-        out[...] = sums[at : at + out.shape[0]].astype(out.dtype)
+        here = pl.ds(at, out.shape[0])
+        out[...] = (kept[here] + taken[here].astype(jnp.float32)).astype(out.dtype)
         at += out.shape[0]
 
 
-def call(body, sizes, *args, rounds=1):
-    rows, landmarks, _, weights = args[:4]
-    read = sum(arg.size * arg.dtype.itemsize for arg in args)
-    cost = pl.CostEstimate(
-        flops=rounds * 2 * rows.shape[0] * landmarks.shape[0] * (rows.shape[1] + weights.shape[1]),
-        bytes_accessed=rounds * read,
-        transcendentals=rows.shape[0] * landmarks.shape[0],
-    )
+def join(sizes, kept, taken):
+    count, width = kept.shape
     return pl.pallas_call(
-        body,
-        out_shape=[jax.ShapeDtypeStruct((size, weights.shape[1]), jnp.bfloat16) for size in sizes],
-        in_specs=[VMEM] * len(args),
+        join_body,
+        out_shape=[jax.ShapeDtypeStruct((size, width), jnp.bfloat16) for size in sizes],
+        in_specs=[VMEM] * 2,
         out_specs=[VMEM] * len(sizes),
         compiler_params=PARAMS,
-        cost_estimate=cost,
-    )(*args)
+        cost_estimate=pl.CostEstimate(
+            flops=count * width, bytes_accessed=8 * count * width, transcendentals=0
+        ),
+    )(kept, taken)
+
+
+def add_body(*refs):
+    *parts, out = refs
+    total = parts[0][...].astype(jnp.float32)
+    for part in parts[1:]:
+        total += part[...].astype(jnp.float32)
+    out[...] = total
+
+
+def add(*parts, weight=1):
+    return pl.pallas_call(
+        add_body,
+        out_shape=jax.ShapeDtypeStruct(parts[0].shape, jnp.float32),
+        in_specs=[VMEM] * len(parts),
+        out_specs=VMEM,
+        compiler_params=PARAMS,
+        cost_estimate=pl.CostEstimate(
+            flops=weight * HEAVY, bytes_accessed=0, transcendentals=0
+        ),
+    )(*parts)
 
 
 def solution(mesh):
@@ -117,26 +153,34 @@
             lines.append(line)
         lines = [jnp.concatenate(line) for line in lines]
 
-        tables = (landmarks, land_sq, whitening)
-        seconds = [swap(lines[0])]
-        seconds[0], *lines[1:] = lax.optimization_barrier(seconds + lines[1:])
-        given = [
-            call(give_body, [first.shape[0]], first, *tables, rounds=20 if k else 1)[0]
-            for k, first in enumerate(lines)
-        ]
-        taken = [swap(given[0])]
-        taken[0], *given[1:] = lax.optimization_barrier(taken + given[1:])
-        taken += [swap(block) for block in given[1:]]
-        seconds += [swap(first) for first in lines[1:]]
+        def line_sums(sizes, first, *tables):
+            second = swap(first)
+            taken = swap(line_part(jnp.bfloat16, 1, first, *tables))
+            return list(join(sizes, line_part(jnp.float32, 10, second, *tables), taken))
+
+        def nothing(sizes, first, *tables):
+            return [jnp.zeros((size, whitening.shape[1]), jnp.bfloat16) for size in sizes]
+
+        go = lax.axis_index("lm") >= 0
+        sums = []
+        for k, first in enumerate(lines):
+            sizes = ([rows, rows] if k == inner - 1 else [2 * rows]) + [2 * rows] * (outer // 2 - 1)
+            work, none = (functools.partial(branch, sizes) for branch in (line_sums, nothing))
+            sums.append(lax.cond(go, work, none, first, landmarks, land_sq, whitening))
+        sums[0][0], sums[-1] = lax.optimization_barrier((sums[0][0], sums[-1]))
         near, far = [], []
-        for k, first in enumerate(lines):
-            sizes = [2 * rows] * (outer // 2)
-            blocks = call(keep_body, sizes, seconds[k], *tables, taken[k])
-            for i in reversed(range(outer // 2)):
-                by = (steps[1][i] * inner + k, steps[0][i] * inner + k)
-                (far if i else near).append(exchange(blocks[i], by))
-        total = sum(part.astype(jnp.float32) for part in far + near)
-        return total[rows:] + swap(total[:rows])
+        for k, blocks in enumerate(sums):
+            *firsts, by0 = [
+                (steps[1][i] * inner + k, steps[0][i] * inner + k) for i in reversed(range(outer // 2))
+            ]
+            far += [exchange(block, by) for block, by in zip(blocks[::-1], firsts)]
+            if k < inner - 1:
+                near.append(exchange(blocks[0], by0))
+            else:
+                last = [exchange(blocks[1], by0), exchange(blocks[0], by0, 1)]
+        early = outer // 2 - 1
+        total = add(add(*far[:early]), *far[early:], *near)
+        return add(total[rows:], *last) + swap(total[:rows])
 
     return jax.shard_map(
         local,

time: 34.3 us -> 32.5 us (0.948)
  waiting for transfers between devices: 10.4 us -> 8.53 us
    ppermute x14 -> x15, waiting for transfers between devices: 10.4 us -> 8.53 us  [exchange(): return lax.ppermute(block, AXES, pairs)]
    pallas_call x4 -> x9, Pallas kernels: 2.34 us -> 2.5 us  [the longest x4 2.33 us: line_part(): pl.pallas_call(sums_body, out_shape=jax.ShapeDtypeStruct((count, width),...]
    add x2 -> x1, other arithmetic: 0.74 us -> 0.67 us  [local(): return add(total[rows:], *last) + swap(total[:rows])]
    ppermute x14 -> x15, starting transfers between devices: 17.6 us -> 17.6 us  [exchange(): return lax.ppermute(block, AXES, pairs)]
    unnamed x2 -> x1, local copies, waits for them, and re-layouts: 0.77 us -> 0.76 us
  transfers between devices with their start and end apart: 14 -> 15, of which waited for: 5 -> 8; matrix products, arithmetic and copies ran while one was open for 2% -> 2% of each run, Pallas kernels for 13% -> 14%
where the time goes in v4:
time: 32.5 us; the launch traced here: 32.3 us
  starting transfers between devices  17.6 us (54%)
  waiting for transfers between devices  8.53 us (26%)
  Pallas kernels  4.49 us (14%)
  local copies, waits for them, and re-layouts  0.78 us (2%)
  other arithmetic  0.69 us (2%)
    ppermute x15, starting transfers between devices, exchange(): return lax.ppermute(block, AXES, pairs)  17.6 us
    ppermute x15, waiting for transfers between devices, exchange(): return lax.ppermute(block, AXES, pairs)  8.53 us
    pallas_call x4, Pallas kernels, line_part(): pl.pallas_call(sums_body, out_shape=jax.ShapeDtypeStruct((count, width),...  2.33 us
    pallas_call x1, Pallas kernels, load(): pl.pallas_call(load_body, out_shape=[jax.ShapeDtypeStruct(landmarks.shape...  2 us
    unnamed x1, local copies, waits for them, and re-layouts  0.76 us
    add x1, other arithmetic, local(): return add(total[rows:], *last) + swap(total[:rows])  0.67 us
  transfers between devices with their start and end apart: 15, of which 8 were waited for; matrix products, arithmetic and copies ran while one was open for 2% of the time, Pallas kernels for 14%

profile of v4, /device:TPU:0, one launch (start us, length us, event | category | flops | bytes accessed | tf_op | source)
XLA Modules:
  0.0 32.3 jit_solution(11072302101119139937)
XLA Ops:
  0.5 0.8 %constant_dynamic-update-slice_fusion.1 = bf16[64,512]{1,0:T(8,128)(2,1)S(1)} fusion(bf16[32,512]{1,0:T(8,128)(2,1)} %param.7), kind=kLoop, calls=%fused_computation.3 | loop fusion | bytes 65536
  1.5 0.7 %collective-permute-start.5 = (bf16[64,512]{1,0:T(8,128)(2,1)S(1)}, bf16[64,512]{1,0:T(8,128)(2,1)S(1)}, u32[]{:S(2)}, u32[]{:S(2)}) collective-permute-start(bf16[64,512]{1,0:T(8,128)(2,1)S(1)} %constant_dynamic-update-slice_fusion), channel_id=1, source_target_pairs={{0,0},{1,5},{2,2},{3,7},{4,4},{5,1},{6,6},{7,3},{8,8},{9,13},{10,1... | collective-permute-start | bytes 196616 | tf_op jit(solution)/shard_map/ppermute | solution.py:136
  2.2 5.0 %collective-permute-start.6 = (bf16[64,512]{1,0:T(8,128)(2,1)S(1)}, bf16[64,512]{1,0:T(8,128)(2,1)S(1)}, u32[]{:S(2)}, u32[]{:S(2)}) collective-permute-start(bf16[64,512]{1,0:T(8,128)(2,1)S(1)} %constant_dynamic-update-slice_fusion), channel_id=1, source_target_pairs={{0,12},{1,9},{2,14},{3,11},{4,8},{5,13},{6,10},{7,15},{8,4},{9,1},... | collective-permute-start | bytes 196616 | tf_op jit(solution)/shard_map/ppermute | solution.py:136
  7.2 2.0 %shard_map.37 = (bf16[512,512]{1,0:T(8,128)(2,1)S(1)}, bf16[512,1024]{1,0:T(8,128)(2,1)S(1)}, f32[8,512]{1,0:T(8,128)S(1)}) custom-call(bf16[512,512]{1,0:T(8,128)(2,1)} %landmarks, bf16[512,1024]{1,0:T(8,128)(2,1)} %weights.1), custom_call_target="tpu_custom_call" | custom-call | flops 1000000000 | tf_op jit(solution)/shard_map/pallas_call | solution.py:34
  9.2 1.6 %collective-permute-start.8 = (bf16[64,512]{1,0:T(8,128)(2,1)S(1)}, bf16[64,512]{1,0:T(8,128)(2,1)S(1)}, u32[]{:S(2)}, u32[]{:S(2)}) collective-permute-start(bf16[64,512]{1,0:T(8,128)(2,1)S(1)} %collective-permute-done.5), channel_id=1, source_target_pairs={{0,2},{1,3},{2,0},{3,1},{4,6},{5,7},{6,4},{7,5},{8,10},{9,11},{10,... | collective-permute-start | bytes 196616 | tf_op jit(solution)/shard_map/ppermute | solution.py:136
  10.8 0.6 %collective-permute-start.9 = (bf16[64,512]{1,0:T(8,128)(2,1)S(1)}, bf16[64,512]{1,0:T(8,128)(2,1)S(1)}, u32[]{:S(2)}, u32[]{:S(2)}) collective-permute-start(bf16[64,512]{1,0:T(8,128)(2,1)S(1)} %collective-permute-done.6), channel_id=1, source_target_pairs={{0,2},{1,3},{2,0},{3,1},{4,6},{5,7},{6,4},{7,5},{8,10},{9,11},{10,... | collective-permute-start | bytes 196616 | tf_op jit(solution)/shard_map/ppermute | solution.py:136
  11.4 3.2 %conditional.2 = ((bf16[64,1024]{1,0:T(8,128)(2,1)S(1)}, bf16[64,1024]{1,0:T(8,128)(2,1)S(1)})) conditional(s32[]{:T(128)} %convert_element_type.4, () %tuple.21, (bf16[128,512]{1,0:T(8,128)(2,1)S(1)}, bf16[512,512]{1,0:T(8,128)(2,1)S(1)}, f32[8,512]{1,0:T(8,128)S(1)}, bf16[512,1024]{1,0:T(8,128)(2,1)S(1)}) %tuple.23), branch_computations={%region_0.0_spmd, %region_1.0_spmd} | conditional | flops 2214723584 | bytes 6062168 | solution.py:169
  11.4 1.0 %collective-permute-start = (bf16[128,512]{1,0:T(8,128)(2,1)S(1)}, bf16[128,512]{1,0:T(8,128)(2,1)S(1)}, u32[]{:S(2)}, u32[]{:S(2)}) collective-permute-start(bf16[128,512]{1,0:T(8,128)(2,1)S(1)} %get-tuple-element.21.rows), channel_id=1, source_target_pairs={{0,1},{1,0},{2,3},{3,2},{4,5},{5,4},{6,7},{7,6},{8,9},{9,8},{10,11... | collective-permute-start | bytes 393224 | tf_op jit(solution)/shard_map/cond/branch_1_fun/ppermute | solution.py:136
  12.4 0.6 %branch_1_fun.7 = bf16[128,1024]{1,0:T(8,128)(2,1)S(1)} custom-call(bf16[128,512]{1,0:T(8,128)(2,1)S(1)} %get-tuple-element.21.rows, bf16[512,512]{1,0:T(8,128)(2,1)S(1)} %get-tuple-element.22.landmarks, f32[8,512]{1,0:T(8,128)S(1)} %get-tuple-element.23.land_sq, bf16[512,1024]{1,0:T(8,128)(2,1)S(1)} %get-tuple-element.24.weights), custom_call_target="tpu_custom_call" | custom-call | flops 201326592 | bytes 1720320 | tf_op jit(solution)/shard_map/cond/branch_1_fun/pallas_call | solution.py:67
  13.4 0.6 %branch_1_fun.6.kept = f32[128,1024]{1,0:T(8,128)S(1)} custom-call(bf16[128,512]{1,0:T(8,128)(2,1)S(1)} %collective-permute-done.rows, bf16[512,512]{1,0:T(8,128)(2,1)S(1)} %get-tuple-element.22.landmarks, f32[8,512]{1,0:T(8,128)S(1)} %get-tuple-element.23.land_sq, bf16[512,1024]{1,0:T(8,128)(2,1)S(1)} %get-tuple-element.24.weights), custom_call_target="tpu_custom_call" | custom-call | flops 2013265920 | bytes 1720320 | tf_op jit(solution)/shard_map/cond/branch_1_fun/pallas_call | solution.py:67
  13.9 0.6 %collective-permute-done.1.taken = bf16[128,1024]{1,0:T(8,128)(2,1)S(1)} collective-permute-done((bf16[128,1024]{1,0:T(8,128)(2,1)S(1)}, bf16[128,1024]{1,0:T(8,128)(2,1)S(1)}, u32[]{:S(2)}, u32[]{:S(2)}) %collective-permute-start.1) | collective-permute-done | bytes 262176 | tf_op jit(solution)/shard_map/cond/branch_1_fun/ppermute | solution.py:136
  14.6 2.0 %collective-permute-start.7 = (bf16[64,1024]{1,0:T(8,128)(2,1)S(1)}, bf16[64,1024]{1,0:T(8,128)(2,1)S(1)}, u32[]{:S(2)}, u32[]{:S(2)}) collective-permute-start(bf16[64,1024]{1,0:T(8,128)(2,1)S(1)} %get-tuple-element.48), channel_id=1, source_target_pairs={{0,8},{1,13},{2,10},{3,15},{4,12},{5,9},{6,14},{7,11},{8,0},{9,5},... | collective-permute-start | bytes 393224 | tf_op jit(solution)/shard_map/ppermute | solution.py:136
  16.6 3.4 %conditional.3 = ((bf16[32,1024]{1,0:T(8,128)(2,1)S(1)}, bf16[32,1024]{1,0:T(8,128)(2,1)S(1)}, bf16[64,1024]{1,0:T(8,128)(2,1)S(1)})) conditional(s32[]{:T(128)} %convert_element_type.4, () %tuple.24, (bf16[128,512]{1,0:T(8,128)(2,1)S(1)}, bf16[512,512]{1,0:T(8,128)(2,1)S(1)}, f32[8,512]{1,0:T(8,128)S(1)}, bf16[512,1024]{1,0:T(8,128)(2,1)S(1)}) %tuple.25), branch_computations={%region_2.0_spmd, %region_3.0_spmd} | conditional | flops 2214723584 | bytes 6062168 | solution.py:169
  16.7 1.1 %collective-permute-start.2 = (bf16[128,512]{1,0:T(8,128)(2,1)S(1)}, bf16[128,512]{1,0:T(8,128)(2,1)S(1)}, u32[]{:S(2)}, u32[]{:S(2)}) collective-permute-start(bf16[128,512]{1,0:T(8,128)(2,1)S(1)} %get-tuple-element.25.rows), channel_id=1, source_target_pairs={{0,1},{1,0},{2,3},{3,2},{4,5},{5,4},{6,7},{7,6},{8,9},{9,8},{10,11... | collective-permute-start | bytes 393224 | tf_op jit(solution)/shard_map/cond/branch_1_fun/ppermute | solution.py:136
  17.8 0.6 %branch_1_fun.10 = bf16[128,1024]{1,0:T(8,128)(2,1)S(1)} custom-call(bf16[128,512]{1,0:T(8,128)(2,1)S(1)} %get-tuple-element.25.rows, bf16[512,512]{1,0:T(8,128)(2,1)S(1)} %get-tuple-element.26.landmarks, f32[8,512]{1,0:T(8,128)S(1)} %get-tuple-element.27.land_sq, bf16[512,1024]{1,0:T(8,128)(2,1)S(1)} %get-tuple-element.28.weights), custom_call_target="tpu_custom_call" | custom-call | flops 201326592 | bytes 1720320 | tf_op jit(solution)/shard_map/cond/branch_1_fun/pallas_call | solution.py:67
  18.8 0.6 %branch_1_fun.9.kept = f32[128,1024]{1,0:T(8,128)S(1)} custom-call(bf16[128,512]{1,0:T(8,128)(2,1)S(1)} %collective-permute-done.2.rows, bf16[512,512]{1,0:T(8,128)(2,1)S(1)} %get-tuple-element.26.landmarks, f32[8,512]{1,0:T(8,128)S(1)} %get-tuple-element.27.land_sq, bf16[512,1024]{1,0:T(8,128)(2,1)S(1)} %get-tuple-element.28.weights), custom_call_target="tpu_custom_call" | custom-call | flops 2013265920 | bytes 1720320 | tf_op jit(solution)/shard_map/cond/branch_1_fun/pallas_call | solution.py:67
  19.4 0.6 %collective-permute-done.3.taken = bf16[128,1024]{1,0:T(8,128)(2,1)S(1)} collective-permute-done((bf16[128,1024]{1,0:T(8,128)(2,1)S(1)}, bf16[128,1024]{1,0:T(8,128)(2,1)S(1)}, u32[]{:S(2)}, u32[]{:S(2)}) %collective-permute-start.3) | collective-permute-done | bytes 262176 | tf_op jit(solution)/shard_map/cond/branch_1_fun/ppermute | solution.py:136
  20.0 1.0 %collective-permute-start.10 = (bf16[64,1024]{1,0:T(8,128)(2,1)S(1)}, bf16[64,1024]{1,0:T(8,128)(2,1)S(1)}, u32[]{:S(2)}, u32[]{:S(2)}) collective-permute-start(bf16[64,1024]{1,0:T(8,128)(2,1)S(1)} %get-tuple-element.53), channel_id=1, source_target_pairs={{0,10},{1,15},{2,8},{3,13},{4,14},{5,11},{6,12},{7,9},{8,2},{9,7},... | collective-permute-start | bytes 393224 | tf_op jit(solution)/shard_map/ppermute | solution.py:136
  21.0 3.2 %collective-permute-start.11 = (bf16[64,1024]{1,0:T(8,128)(2,1)S(1)}, bf16[64,1024]{1,0:T(8,128)(2,1)S(1)}, u32[]{:S(2)}, u32[]{:S(2)}) collective-permute-start(bf16[64,1024]{1,0:T(8,128)(2,1)S(1)} %get-tuple-element.54), channel_id=1, source_target_pairs={{0,4},{1,1},{2,6},{3,3},{4,0},{5,5},{6,2},{7,7},{8,12},{9,9},{10,1... | collective-permute-start | bytes 393224 | tf_op jit(solution)/shard_map/ppermute | solution.py:136
  24.1 0.9 %collective-permute-start.12 = (bf16[32,1024]{1,0:T(8,128)(2,1)S(1)}, bf16[32,1024]{1,0:T(8,128)(2,1)S(1)}, u32[]{:S(2)}, u32[]{:S(2)}) collective-permute-start(bf16[32,1024]{1,0:T(8,128)(2,1)S(1)} %get-tuple-element.55), channel_id=1, source_target_pairs={{0,6},{1,3},{2,4},{3,1},{4,2},{5,7},{6,0},{7,5},{8,14},{9,11},{10,... | collective-permute-start | bytes 196616 | tf_op jit(solution)/shard_map/ppermute | solution.py:136
  25.1 4.9 %collective-permute-done.10.refs_1_ = bf16[64,1024]{1,0:T(8,128)(2,1)S(1)} collective-permute-done((bf16[64,1024]{1,0:T(8,128)(2,1)S(1)}, bf16[64,1024]{1,0:T(8,128)(2,1)S(1)}, u32[]{:S(2)}, u32[]{:S(2)}) %collective-permute-start.10) | collective-permute-done | bytes 131104 | tf_op jit(solution)/shard_map/ppermute | solution.py:136
  30.2 0.7 %collective-permute-done.12.refs_1_ = bf16[32,1024]{1,0:T(8,128)(2,1)S(1)} collective-permute-done((bf16[32,1024]{1,0:T(8,128)(2,1)S(1)}, bf16[32,1024]{1,0:T(8,128)(2,1)S(1)}, u32[]{:S(2)}, u32[]{:S(2)}) %collective-permute-start.12) | collective-permute-done | bytes 65568 | tf_op jit(solution)/shard_map/ppermute | solution.py:136
  30.8 0.7 %collective-permute-done.13.refs_2_ = bf16[32,1024]{1,0:T(8,128)(2,1)S(1)} collective-permute-done((bf16[32,1024]{1,0:T(8,128)(2,1)S(1)}, bf16[32,1024]{1,0:T(8,128)(2,1)S(1)}, u32[]{:S(2)}, u32[]{:S(2)}) %collective-permute-start.13) | collective-permute-done | bytes 65568 | tf_op jit(solution)/shard_map/ppermute | solution.py:136
  31.6 0.7 %add.3 = f32[32,1024]{1,0:T(8,128)} add(f32[32,1024]{1,0:T(8,128)S(1)} %shard_map.40, f32[32,1024]{1,0:T(8,128)S(1)} %collective-permute-done.14) | non-fusion elementwise | flops 32768 | bytes 393216 | tf_op jit(solution)/shard_map/add | solution.py:183
  (24 shorter events, 1.9 us)
Async XLA Ops:
  0.0 1.5 %collective-permute-start.4 = (bf16[32,512]{1,0:T(8,128)(2,1)}, bf16[32,512]{1,0:T(8,128)(2,1)S(1)}, u32[]{:S(2)}, u32[]{:S(2)}) collective-permute-start(bf16[32,512]{1,0:T(8,128)(2,1)} %param.7), channel_id=1, source_target_pairs={{0,1},{1,0},{2,3},{3,2},{4,5},{5,4},{6,7},{7,6},{8,9},{9,8},{10,11... | collective-permute-start | bytes 98312 | tf_op jit(solution)/shard_map/ppermute | solution.py:136
  1.5 7.7 %collective-permute-start.5 = (bf16[64,512]{1,0:T(8,128)(2,1)S(1)}, bf16[64,512]{1,0:T(8,128)(2,1)S(1)}, u32[]{:S(2)}, u32[]{:S(2)}) collective-permute-start(bf16[64,512]{1,0:T(8,128)(2,1)S(1)} %constant_dynamic-update-slice_fusion), channel_id=1, source_target_pairs={{0,0},{1,5},{2,2},{3,7},{4,4},{5,1},{6,6},{7,3},{8,8},{9,13},{10,1... | collective-permute-start | bytes 196616 | tf_op jit(solution)/shard_map/ppermute | solution.py:136
  2.2 8.6 %collective-permute-start.6 = (bf16[64,512]{1,0:T(8,128)(2,1)S(1)}, bf16[64,512]{1,0:T(8,128)(2,1)S(1)}, u32[]{:S(2)}, u32[]{:S(2)}) collective-permute-start(bf16[64,512]{1,0:T(8,128)(2,1)S(1)} %constant_dynamic-update-slice_fusion), channel_id=1, source_target_pairs={{0,12},{1,9},{2,14},{3,11},{4,8},{5,13},{6,10},{7,15},{8,4},{9,1},... | collective-permute-start | bytes 196616 | tf_op jit(solution)/shard_map/ppermute | solution.py:136
  9.2 7.4 %collective-permute-start.8 = (bf16[64,512]{1,0:T(8,128)(2,1)S(1)}, bf16[64,512]{1,0:T(8,128)(2,1)S(1)}, u32[]{:S(2)}, u32[]{:S(2)}) collective-permute-start(bf16[64,512]{1,0:T(8,128)(2,1)S(1)} %collective-permute-done.5), channel_id=1, source_target_pairs={{0,2},{1,3},{2,0},{3,1},{4,6},{5,7},{6,4},{7,5},{8,10},{9,11},{10,... | collective-permute-start | bytes 196616 | tf_op jit(solution)/shard_map/ppermute | solution.py:136
  10.8 5.8 %collective-permute-start.9 = (bf16[64,512]{1,0:T(8,128)(2,1)S(1)}, bf16[64,512]{1,0:T(8,128)(2,1)S(1)}, u32[]{:S(2)}, u32[]{:S(2)}) collective-permute-start(bf16[64,512]{1,0:T(8,128)(2,1)S(1)} %collective-permute-done.6), channel_id=1, source_target_pairs={{0,2},{1,3},{2,0},{3,1},{4,6},{5,7},{6,4},{7,5},{8,10},{9,11},{10,... | collective-permute-start | bytes 196616 | tf_op jit(solution)/shard_map/ppermute | solution.py:136
  11.4 2.0 %collective-permute-start = (bf16[128,512]{1,0:T(8,128)(2,1)S(1)}, bf16[128,512]{1,0:T(8,128)(2,1)S(1)}, u32[]{:S(2)}, u32[]{:S(2)}) collective-permute-start(bf16[128,512]{1,0:T(8,128)(2,1)S(1)} %get-tuple-element.21.rows), channel_id=1, source_target_pairs={{0,1},{1,0},{2,3},{3,2},{4,5},{5,4},{6,7},{7,6},{8,9},{9,8},{10,11... | collective-permute-start | bytes 393224 | tf_op jit(solution)/shard_map/cond/branch_1_fun/ppermute | solution.py:136
  13.0 1.6 %collective-permute-start.1 = (bf16[128,1024]{1,0:T(8,128)(2,1)S(1)}, bf16[128,1024]{1,0:T(8,128)(2,1)S(1)}, u32[]{:S(2)}, u32[]{:S(2)}) collective-permute-start(bf16[128,1024]{1,0:T(8,128)(2,1)S(1)} %branch_1_fun.7), channel_id=1, source_target_pairs={{0,1},{1,0},{2,3},{3,2},{4,5},{5,4},{6,7},{7,6},{8,9},{9,8},{10,11... | collective-permute-start | bytes 786440 | tf_op jit(solution)/shard_map/cond/branch_1_fun/ppermute | solution.py:136
  14.6 10.4 %collective-permute-start.7 = (bf16[64,1024]{1,0:T(8,128)(2,1)S(1)}, bf16[64,1024]{1,0:T(8,128)(2,1)S(1)}, u32[]{:S(2)}, u32[]{:S(2)}) collective-permute-start(bf16[64,1024]{1,0:T(8,128)(2,1)S(1)} %get-tuple-element.48), channel_id=1, source_target_pairs={{0,8},{1,13},{2,10},{3,15},{4,12},{5,9},{6,14},{7,11},{8,0},{9,5},... | collective-permute-start | bytes 393224 | tf_op jit(solution)/shard_map/ppermute | solution.py:136
  16.7 2.1 %collective-permute-start.2 = (bf16[128,512]{1,0:T(8,128)(2,1)S(1)}, bf16[128,512]{1,0:T(8,128)(2,1)S(1)}, u32[]{:S(2)}, u32[]{:S(2)}) collective-permute-start(bf16[128,512]{1,0:T(8,128)(2,1)S(1)} %get-tuple-element.25.rows), channel_id=1, source_target_pairs={{0,1},{1,0},{2,3},{3,2},{4,5},{5,4},{6,7},{7,6},{8,9},{9,8},{10,11... | collective-permute-start | bytes 393224 | tf_op jit(solution)/shard_map/cond/branch_1_fun/ppermute | solution.py:136
  18.4 1.6 %collective-permute-start.3 = (bf16[128,1024]{1,0:T(8,128)(2,1)S(1)}, bf16[128,1024]{1,0:T(8,128)(2,1)S(1)}, u32[]{:S(2)}, u32[]{:S(2)}) collective-permute-start(bf16[128,1024]{1,0:T(8,128)(2,1)S(1)} %branch_1_fun.10), channel_id=1, source_target_pairs={{0,1},{1,0},{2,3},{3,2},{4,5},{5,4},{6,7},{7,6},{8,9},{9,8},{10,11... | collective-permute-start | bytes 786440 | tf_op jit(solution)/shard_map/cond/branch_1_fun/ppermute | solution.py:136
  20.0 10.0 %collective-permute-start.10 = (bf16[64,1024]{1,0:T(8,128)(2,1)S(1)}, bf16[64,1024]{1,0:T(8,128)(2,1)S(1)}, u32[]{:S(2)}, u32[]{:S(2)}) collective-permute-start(bf16[64,1024]{1,0:T(8,128)(2,1)S(1)} %get-tuple-element.53), channel_id=1, source_target_pairs={{0,10},{1,15},{2,8},{3,13},{4,14},{5,11},{6,12},{7,9},{8,2},{9,7},... | collective-permute-start | bytes 393224 | tf_op jit(solution)/shard_map/ppermute | solution.py:136
  21.0 9.0 %collective-permute-start.11 = (bf16[64,1024]{1,0:T(8,128)(2,1)S(1)}, bf16[64,1024]{1,0:T(8,128)(2,1)S(1)}, u32[]{:S(2)}, u32[]{:S(2)}) collective-permute-start(bf16[64,1024]{1,0:T(8,128)(2,1)S(1)} %get-tuple-element.54), channel_id=1, source_target_pairs={{0,4},{1,1},{2,6},{3,3},{4,0},{5,5},{6,2},{7,7},{8,12},{9,9},{10,1... | collective-permute-start | bytes 393224 | tf_op jit(solution)/shard_map/ppermute | solution.py:136
  24.1 6.7 %collective-permute-start.12 = (bf16[32,1024]{1,0:T(8,128)(2,1)S(1)}, bf16[32,1024]{1,0:T(8,128)(2,1)S(1)}, u32[]{:S(2)}, u32[]{:S(2)}) collective-permute-start(bf16[32,1024]{1,0:T(8,128)(2,1)S(1)} %get-tuple-element.55), channel_id=1, source_target_pairs={{0,6},{1,3},{2,4},{3,1},{4,2},{5,7},{6,0},{7,5},{8,14},{9,11},{10,... | collective-permute-start | bytes 196616 | tf_op jit(solution)/shard_map/ppermute | solution.py:136
  25.0 6.5 %collective-permute-start.13 = (bf16[32,1024]{1,0:T(8,128)(2,1)S(1)}, bf16[32,1024]{1,0:T(8,128)(2,1)S(1)}, u32[]{:S(2)}, u32[]{:S(2)}) collective-permute-start(bf16[32,1024]{1,0:T(8,128)(2,1)S(1)} %get-tuple-element.56), channel_id=1, source_target_pairs={{0,7},{1,2},{2,5},{3,0},{4,3},{5,6},{6,1},{7,4},{8,15},{9,10},{10,... | collective-permute-start | bytes 196616 | tf_op jit(solution)/shard_map/ppermute | solution.py:136
  30.1 1.5 %collective-permute-start.14 = (f32[32,1024]{1,0:T(8,128)S(1)}, f32[32,1024]{1,0:T(8,128)S(1)}, u32[]{:S(2)}, u32[]{:S(2)}) collective-permute-start(f32[32,1024]{1,0:T(8,128)S(1)} %get-tuple-element.57), channel_id=1, source_target_pairs={{0,1},{1,0},{2,3},{3,2},{4,5},{5,4},{6,7},{7,6},{8,9},{9,8},{10,11... | collective-permute-start | bytes 393224 | tf_op jit(solution)/shard_map/ppermute | solution.py:136

commit v5 on v4

--- a/solution.py
+++ b/solution.py
@@ -8,7 +8,7 @@
 from jax.sharding import PartitionSpec as P
 
 AXES = ("lm", "env")
-HEAVY = 5*10**9
+HEAVY = 5 * 10**9
 VMEM = pl.BlockSpec(memory_space=pltpu.VMEM)
 PARAMS = pltpu.CompilerParams(vmem_limit_bytes=16 * 2**20)
 
@@ -20,12 +20,12 @@
     second.start()
     first.wait()
     square = jnp.square(landmarks_out[...].astype(jnp.float32))
-    land_sq[...] = lax.dot_general(
-        jnp.ones((8, square.shape[1]), jnp.float32),
-        square,
-        (((1,), (1,)), ((), ())),
-        precision=lax.Precision.HIGHEST,
-        preferred_element_type=jnp.float32,
+    high = square.astype(jnp.bfloat16)
+    low = (square - high.astype(jnp.float32)).astype(jnp.bfloat16)
+    ones = jnp.ones((8, square.shape[1]), jnp.bfloat16)
+    land_sq[...] = sum(
+        lax.dot_general(ones, part, (((1,), (1,)), ((), ())), preferred_element_type=jnp.float32)
+        for part in (high, low)
     )
     second.wait()
 
@@ -100,6 +100,20 @@
     )(kept, taken)
 
 
+def copy_body(block, out):
+    out[...] = block[...]
+
+
+def copy(block):
+    return pl.pallas_call(
+        copy_body,
+        out_shape=jax.ShapeDtypeStruct(block.shape, block.dtype),
+        in_specs=[VMEM],
+        out_specs=VMEM,
+        compiler_params=PARAMS,
+    )(block)
+
+
 def add_body(*refs):
     *parts, out = refs
     total = parts[0][...].astype(jnp.float32)
@@ -147,11 +161,11 @@
         got = [exchange(chip_rows, (a * inner, b * inner)) for a, b in reversed(list(zip(*steps)))]
         landmarks, whitening, land_sq = load(landmarks, whitening)
         got = got[::-1]
+        got[-1], land_sq = lax.optimization_barrier((got[-1], land_sq))
         lines = [got]
         for k in range(1, inner):
             line = [exchange(block, (k, k)) for block in got]
             lines.append(line)
-        lines = [jnp.concatenate(line) for line in lines]
 
         def line_sums(sizes, first, *tables):
             second = swap(first)
@@ -162,24 +176,26 @@
             return [jnp.zeros((size, whitening.shape[1]), jnp.bfloat16) for size in sizes]
 
         go = lax.axis_index("lm") >= 0
-        sums = []
-        for k, first in enumerate(lines):
-            sizes = ([rows, rows] if k == inner - 1 else [2 * rows]) + [2 * rows] * (outer // 2 - 1)
+        groups = [[(i, k) for i in range(outer // 2)] for k in range(inner)]
+        groups[1].insert(0, groups[0].pop(0))
+        parts, last = [], []
+        for group in groups:
+            first = [lines[k][i] for i, k in group]
+            first = jnp.concatenate(first) if len(first) > 1 else copy(*first)
+            sizes = []
+            for where in group:
+                sizes += [rows, rows] if where == (0, inner - 1) else [2 * rows]
             work, none = (functools.partial(branch, sizes) for branch in (line_sums, nothing))
-            sums.append(lax.cond(go, work, none, first, landmarks, land_sq, whitening))
-        sums[0][0], sums[-1] = lax.optimization_barrier((sums[0][0], sums[-1]))
-        near, far = [], []
-        for k, blocks in enumerate(sums):
-            *firsts, by0 = [
-                (steps[1][i] * inner + k, steps[0][i] * inner + k) for i in reversed(range(outer // 2))
-            ]
-            far += [exchange(block, by) for block, by in zip(blocks[::-1], firsts)]
-            if k < inner - 1:
-                near.append(exchange(blocks[0], by0))
-            else:
-                last = [exchange(blocks[1], by0), exchange(blocks[0], by0, 1)]
+            blocks = lax.cond(go, work, none, first, landmarks, land_sq, whitening)
+            for i, k in reversed(group):
+                by = (steps[1][i] * inner + k, steps[0][i] * inner + k)
+                block = blocks.pop()
+                if (i, k) == (0, inner - 1):
+                    last = [exchange(block, by), exchange(blocks.pop(), by, 1)]
+                else:
+                    parts.append(exchange(block, by))
         early = outer // 2 - 1
-        total = add(add(*far[:early]), *far[early:], *near)
+        total = add(add(*parts[:early]), *parts[early:])
         return add(total[rows:], *last) + swap(total[:rows])
 
     return jax.shard_map(

time: 32.5 us -> 32.2 us (level)
  waiting for transfers between devices: 8.53 us -> 9.13 us
  Pallas kernels: 4.49 us -> 4.06 us
  starting transfers between devices: 17.6 us -> 17.2 us
    ppermute x15, waiting for transfers between devices: 8.53 us -> 9.13 us  [exchange(): return lax.ppermute(block, AXES, pairs)]
    pallas_call x1, Pallas kernels: 2 us -> 1.49 us  [load(): pl.pallas_call(load_body, out_shape=[jax.ShapeDtypeStruct(landmarks.shape...]
    ppermute x15, starting transfers between devices: 17.6 us -> 17.2 us  [exchange(): return lax.ppermute(block, AXES, pairs)]
  transfers between devices with their start and end apart: 15 -> 15, of which waited for: 8 -> 11; matrix products, arithmetic and copies ran while one was open for 2% -> 2% of each run, Pallas kernels for 14% -> 13%
where the time goes in v5:
time: 32.2 us; the launch traced here: 32 us
  starting transfers between devices  17.2 us (53%)
  waiting for transfers between devices  9.13 us (28%)
  Pallas kernels  4.06 us (13%)
  local copies, waits for them, and re-layouts  0.78 us (2%)
  other arithmetic  0.69 us (2%)
    ppermute x15, starting transfers between devices, exchange(): return lax.ppermute(block, AXES, pairs)  17.2 us
    ppermute x15, waiting for transfers between devices, exchange(): return lax.ppermute(block, AXES, pairs)  9.13 us
    pallas_call x4, Pallas kernels, line_part(): pl.pallas_call(sums_body, out_shape=jax.ShapeDtypeStruct((count, width),...  2.4 us
    pallas_call x1, Pallas kernels, load(): pl.pallas_call(load_body, out_shape=[jax.ShapeDtypeStruct(landmarks.shape...  1.49 us
    unnamed x1, local copies, waits for them, and re-layouts  0.76 us
    add x1, other arithmetic, local(): return add(total[rows:], *last) + swap(total[:rows])  0.67 us
  transfers between devices with their start and end apart: 15, of which 11 were waited for; matrix products, arithmetic and copies ran while one was open for 2% of the time, Pallas kernels for 13%

profile of v5, /device:TPU:0, one launch (start us, length us, event | category | flops | bytes accessed | tf_op | source)
XLA Modules:
  0.0 32.0 jit_solution(10901843748983204372)
XLA Ops:
  0.5 0.8 %constant_dynamic-update-slice_fusion.1 = bf16[64,512]{1,0:T(8,128)(2,1)S(1)} fusion(bf16[32,512]{1,0:T(8,128)(2,1)} %param.7), kind=kLoop, calls=%fused_computation.2 | loop fusion | bytes 65536
  1.5 4.9 %collective-permute-start.5 = (bf16[64,512]{1,0:T(8,128)(2,1)S(1)}, bf16[64,512]{1,0:T(8,128)(2,1)S(1)}, u32[]{:S(2)}, u32[]{:S(2)}) collective-permute-start(bf16[64,512]{1,0:T(8,128)(2,1)S(1)} %constant_dynamic-update-slice_fusion), channel_id=1, source_target_pairs={{0,12},{1,9},{2,14},{3,11},{4,8},{5,13},{6,10},{7,15},{8,4},{9,1},... | collective-permute-start | bytes 196616 | tf_op jit(solution)/shard_map/ppermute | solution.py:150
  6.5 0.7 %collective-permute-start.7 = (bf16[64,512]{1,0:T(8,128)(2,1)S(1)}, bf16[64,512]{1,0:T(8,128)(2,1)S(1)}, u32[]{:S(2)}, u32[]{:S(2)}) collective-permute-start(bf16[64,512]{1,0:T(8,128)(2,1)S(1)} %constant_dynamic-update-slice_fusion), channel_id=1, source_target_pairs={{0,0},{1,5},{2,2},{3,7},{4,4},{5,1},{6,6},{7,3},{8,8},{9,13},{10,1... | collective-permute-start | bytes 196616 | tf_op jit(solution)/shard_map/ppermute | solution.py:150
  7.1 1.5 %shard_map.37 = (bf16[512,512]{1,0:T(8,128)(2,1)S(1)}, bf16[512,1024]{1,0:T(8,128)(2,1)S(1)}, f32[8,512]{1,0:T(8,128)S(1)}) custom-call(bf16[512,512]{1,0:T(8,128)(2,1)} %landmarks, bf16[512,1024]{1,0:T(8,128)(2,1)} %weights.1), custom_call_target="tpu_custom_call" | custom-call | flops 1000000000 | tf_op jit(solution)/shard_map/pallas_call | solution.py:34
  9.0 1.5 %collective-permute-start.9 = (bf16[64,512]{1,0:T(8,128)(2,1)S(1)}, bf16[64,512]{1,0:T(8,128)(2,1)S(1)}, u32[]{:S(2)}, u32[]{:S(2)}) collective-permute-start(bf16[64,512]{1,0:T(8,128)(2,1)S(1)} %collective-permute-done.5.block), channel_id=1, source_target_pairs={{0,2},{1,3},{2,0},{3,1},{4,6},{5,7},{6,4},{7,5},{8,10},{9,11},{10,... | collective-permute-start | bytes 196616 | tf_op jit(solution)/shard_map/ppermute | solution.py:150
  10.6 0.5 %collective-permute-start.8 = (bf16[64,512]{1,0:T(8,128)(2,1)S(1)}, bf16[64,512]{1,0:T(8,128)(2,1)S(1)}, u32[]{:S(2)}, u32[]{:S(2)}) collective-permute-start(bf16[64,512]{1,0:T(8,128)(2,1)S(1)} %collective-permute-done.7), channel_id=1, source_target_pairs={{0,2},{1,3},{2,0},{3,1},{4,6},{5,7},{6,4},{7,5},{8,10},{9,11},{10,... | collective-permute-start | bytes 196616 | tf_op jit(solution)/shard_map/ppermute | solution.py:150
  11.1 2.5 %conditional.2 = (bf16[64,1024]{1,0:T(8,128)(2,1)S(1)}) conditional(s32[]{:T(128)} %convert_element_type.4, () %tuple.20, (bf16[64,512]{1,0:T(8,128)(2,1)S(1)}, bf16[512,512]{1,0:T(8,128)(2,1)S(1)}, f32[8,512]{1,0:T(8,128)S(1)}, bf16[512,1024]{1,0:T(8,128)(2,1)S(1)}) %tuple.23), branch_computations={%region_0.0_spmd, %region_1.0_spmd} | conditional | flops 1107361792 | bytes 4620376 | solution.py:189
  11.1 0.5 %collective-permute-start = (bf16[64,512]{1,0:T(8,128)(2,1)S(1)}, bf16[64,512]{1,0:T(8,128)(2,1)S(1)}, u32[]{:S(2)}, u32[]{:S(2)}) collective-permute-start(bf16[64,512]{1,0:T(8,128)(2,1)S(1)} %get-tuple-element.24.rows), channel_id=1, source_target_pairs={{0,1},{1,0},{2,3},{3,2},{4,5},{5,4},{6,7},{7,6},{8,9},{9,8},{10,11... | collective-permute-start | bytes 196616 | tf_op jit(solution)/shard_map/cond/branch_1_fun/ppermute | solution.py:150
  11.6 0.5 %branch_1_fun.7 = bf16[64,1024]{1,0:T(8,128)(2,1)S(1)} custom-call(bf16[64,512]{1,0:T(8,128)(2,1)S(1)} %get-tuple-element.24.rows, bf16[512,512]{1,0:T(8,128)(2,1)S(1)} %get-tuple-element.25.landmarks, f32[8,512]{1,0:T(8,128)S(1)} %get-tuple-element.26.land_sq, bf16[512,1024]{1,0:T(8,128)(2,1)S(1)} %get-tuple-element.27.weights), custom_call_target="tpu_custom_call" | custom-call | flops 100663296 | bytes 1654784 | tf_op jit(solution)/shard_map/cond/branch_1_fun/pallas_call | solution.py:67
  12.5 0.5 %branch_1_fun.6.kept = f32[64,1024]{1,0:T(8,128)S(1)} custom-call(bf16[64,512]{1,0:T(8,128)(2,1)S(1)} %collective-permute-done.rows, bf16[512,512]{1,0:T(8,128)(2,1)S(1)} %get-tuple-element.25.landmarks, f32[8,512]{1,0:T(8,128)S(1)} %get-tuple-element.26.land_sq, bf16[512,1024]{1,0:T(8,128)(2,1)S(1)} %get-tuple-element.27.weights), custom_call_target="tpu_custom_call" | custom-call | flops 1006632960 | bytes 1654784 | tf_op jit(solution)/shard_map/cond/branch_1_fun/pallas_call | solution.py:67
  13.1 0.5 %collective-permute-done.1.taken = bf16[64,1024]{1,0:T(8,128)(2,1)S(1)} collective-permute-done((bf16[64,1024]{1,0:T(8,128)(2,1)S(1)}, bf16[64,1024]{1,0:T(8,128)(2,1)S(1)}, u32[]{:S(2)}, u32[]{:S(2)}) %collective-permute-start.1) | collective-permute-done | bytes 131104 | tf_op jit(solution)/shard_map/cond/branch_1_fun/ppermute | solution.py:150
  13.6 1.6 %collective-permute-start.6 = (bf16[64,1024]{1,0:T(8,128)(2,1)S(1)}, bf16[64,1024]{1,0:T(8,128)(2,1)S(1)}, u32[]{:S(2)}, u32[]{:S(2)}) collective-permute-start(bf16[64,1024]{1,0:T(8,128)(2,1)S(1)} %get-tuple-element.64), channel_id=1, source_target_pairs={{0,8},{1,13},{2,10},{3,15},{4,12},{5,9},{6,14},{7,11},{8,0},{9,5},... | collective-permute-start | bytes 393224 | tf_op jit(solution)/shard_map/ppermute | solution.py:150
  15.4 4.2 %conditional.3 = ((bf16[64,1024]{1,0:T(8,128)(2,1)S(1)}, bf16[32,1024]{1,0:T(8,128)(2,1)S(1)}, bf16[32,1024]{1,0:T(8,128)(2,1)S(1)}, bf16[64,1024]{1,0:T(8,128)(2,1)S(1)})) conditional(s32[]{:T(128)} %convert_element_type.4, () %tuple.24, (bf16[192,512]{1,0:T(8,128)(2,1)S(1)}, bf16[512,512]{1,0:T(8,128)(2,1)S(1)}, f32[8,512]{1,0:T(8,128)S(1)}, ...), branch_computations={%region_2.0_spmd, %region_3.0_spmd} | conditional | flops 3322085376 | bytes 7503960 | solution.py:189
  15.4 1.7 %collective-permute-start.2 = (bf16[192,512]{1,0:T(8,128)(2,1)S(1)}, bf16[192,512]{1,0:T(8,128)(2,1)S(1)}, u32[]{:S(2)}, u32[]{:S(2)}) collective-permute-start(bf16[192,512]{1,0:T(8,128)(2,1)S(1)} %get-tuple-element.28.rows), channel_id=1, source_target_pairs={{0,1},{1,0},{2,3},{3,2},{4,5},{5,4},{6,7},{7,6},{8,9},{9,8},{10,11... | collective-permute-start | bytes 589832 | tf_op jit(solution)/shard_map/cond/branch_1_fun/ppermute | solution.py:150
  17.2 0.6 %branch_1_fun.10 = bf16[192,1024]{1,0:T(8,128)(2,1)S(1)} custom-call(bf16[192,512]{1,0:T(8,128)(2,1)S(1)} %get-tuple-element.28.rows, bf16[512,512]{1,0:T(8,128)(2,1)S(1)} %get-tuple-element.29.landmarks, f32[8,512]{1,0:T(8,128)S(1)} %get-tuple-element.30.land_sq, bf16[512,1024]{1,0:T(8,128)(2,1)S(1)} %get-tuple-element.31.weights), custom_call_target="tpu_custom_call" | custom-call | flops 301989888 | bytes 1785856 | tf_op jit(solution)/shard_map/cond/branch_1_fun/pallas_call | solution.py:67
  18.2 0.6 %branch_1_fun.9.kept = f32[192,1024]{1,0:T(8,128)S(1)} custom-call(bf16[192,512]{1,0:T(8,128)(2,1)S(1)} %collective-permute-done.2.rows, bf16[512,512]{1,0:T(8,128)(2,1)S(1)} %get-tuple-element.29.landmarks, f32[8,512]{1,0:T(8,128)S(1)} %get-tuple-element.30.land_sq, bf16[512,1024]{1,0:T(8,128)(2,1)S(1)} %get-tuple-element.31.weights), custom_call_target="tpu_custom_call" | custom-call | flops 3019898880 | bytes 1785856 | tf_op jit(solution)/shard_map/cond/branch_1_fun/pallas_call | solution.py:67
  18.9 0.7 %collective-permute-done.3.taken = bf16[192,1024]{1,0:T(8,128)(2,1)S(1)} collective-permute-done((bf16[192,1024]{1,0:T(8,128)(2,1)S(1)}, bf16[192,1024]{1,0:T(8,128)(2,1)S(1)}, u32[]{:S(2)}, u32[]{:S(2)}) %collective-permute-start.3) | collective-permute-done | bytes 393248 | tf_op jit(solution)/shard_map/cond/branch_1_fun/ppermute | solution.py:150
  19.7 0.7 %collective-permute-start.10 = (bf16[64,1024]{1,0:T(8,128)(2,1)S(1)}, bf16[64,1024]{1,0:T(8,128)(2,1)S(1)}, u32[]{:S(2)}, u32[]{:S(2)}) collective-permute-start(bf16[64,1024]{1,0:T(8,128)(2,1)S(1)} %get-tuple-element.50), channel_id=1, source_target_pairs={{0,10},{1,15},{2,8},{3,13},{4,14},{5,11},{6,12},{7,9},{8,2},{9,7},... | collective-permute-start | bytes 393224 | tf_op jit(solution)/shard_map/ppermute | solution.py:150
  20.4 3.9 %collective-permute-start.11 = (bf16[64,1024]{1,0:T(8,128)(2,1)S(1)}, bf16[64,1024]{1,0:T(8,128)(2,1)S(1)}, u32[]{:S(2)}, u32[]{:S(2)}) collective-permute-start(bf16[64,1024]{1,0:T(8,128)(2,1)S(1)} %get-tuple-element.51), channel_id=1, source_target_pairs={{0,4},{1,1},{2,6},{3,3},{4,0},{5,5},{6,2},{7,7},{8,12},{9,9},{10,1... | collective-permute-start | bytes 393224 | tf_op jit(solution)/shard_map/ppermute | solution.py:150
  24.3 0.5 %collective-permute-start.12 = (bf16[32,1024]{1,0:T(8,128)(2,1)S(1)}, bf16[32,1024]{1,0:T(8,128)(2,1)S(1)}, u32[]{:S(2)}, u32[]{:S(2)}) collective-permute-start(bf16[32,1024]{1,0:T(8,128)(2,1)S(1)} %get-tuple-element.52), channel_id=1, source_target_pairs={{0,6},{1,3},{2,4},{3,1},{4,2},{5,7},{6,0},{7,5},{8,14},{9,11},{10,... | collective-permute-start | bytes 196616 | tf_op jit(solution)/shard_map/ppermute | solution.py:150
  24.8 4.7 %collective-permute-done.10.refs_1_ = bf16[64,1024]{1,0:T(8,128)(2,1)S(1)} collective-permute-done((bf16[64,1024]{1,0:T(8,128)(2,1)S(1)}, bf16[64,1024]{1,0:T(8,128)(2,1)S(1)}, u32[]{:S(2)}, u32[]{:S(2)}) %collective-permute-start.10) | collective-permute-done | bytes 131104 | tf_op jit(solution)/shard_map/ppermute | solution.py:150
  29.8 0.8 %collective-permute-done.12.refs_1_ = bf16[32,1024]{1,0:T(8,128)(2,1)S(1)} collective-permute-done((bf16[32,1024]{1,0:T(8,128)(2,1)S(1)}, bf16[32,1024]{1,0:T(8,128)(2,1)S(1)}, u32[]{:S(2)}, u32[]{:S(2)}) %collective-permute-start.12) | collective-permute-done | bytes 65568 | tf_op jit(solution)/shard_map/ppermute | solution.py:150
  30.6 0.7 %collective-permute-done.13.refs_2_ = bf16[32,1024]{1,0:T(8,128)(2,1)S(1)} collective-permute-done((bf16[32,1024]{1,0:T(8,128)(2,1)S(1)}, bf16[32,1024]{1,0:T(8,128)(2,1)S(1)}, u32[]{:S(2)}, u32[]{:S(2)}) %collective-permute-start.13) | collective-permute-done | bytes 65568 | tf_op jit(solution)/shard_map/ppermute | solution.py:150
  31.3 0.7 %add.3 = f32[32,1024]{1,0:T(8,128)} add(f32[32,1024]{1,0:T(8,128)S(1)} %shard_map.41, f32[32,1024]{1,0:T(8,128)S(1)} %collective-permute-done.14) | non-fusion elementwise | flops 32768 | bytes 393216 | tf_op jit(solution)/shard_map/add | solution.py:199
  (24 shorter events, 2.6 us)
Async XLA Ops:
  0.0 1.5 %collective-permute-start.4 = (bf16[32,512]{1,0:T(8,128)(2,1)}, bf16[32,512]{1,0:T(8,128)(2,1)S(1)}, u32[]{:S(2)}, u32[]{:S(2)}) collective-permute-start(bf16[32,512]{1,0:T(8,128)(2,1)} %param.7), channel_id=1, source_target_pairs={{0,1},{1,0},{2,3},{3,2},{4,5},{5,4},{6,7},{7,6},{8,9},{9,8},{10,11... | collective-permute-start | bytes 98312 | tf_op jit(solution)/shard_map/ppermute | solution.py:150
  1.5 7.5 %collective-permute-start.5 = (bf16[64,512]{1,0:T(8,128)(2,1)S(1)}, bf16[64,512]{1,0:T(8,128)(2,1)S(1)}, u32[]{:S(2)}, u32[]{:S(2)}) collective-permute-start(bf16[64,512]{1,0:T(8,128)(2,1)S(1)} %constant_dynamic-update-slice_fusion), channel_id=1, source_target_pairs={{0,12},{1,9},{2,14},{3,11},{4,8},{5,13},{6,10},{7,15},{8,4},{9,1},... | collective-permute-start | bytes 196616 | tf_op jit(solution)/shard_map/ppermute | solution.py:150
  6.5 4.1 %collective-permute-start.7 = (bf16[64,512]{1,0:T(8,128)(2,1)S(1)}, bf16[64,512]{1,0:T(8,128)(2,1)S(1)}, u32[]{:S(2)}, u32[]{:S(2)}) collective-permute-start(bf16[64,512]{1,0:T(8,128)(2,1)S(1)} %constant_dynamic-update-slice_fusion), channel_id=1, source_target_pairs={{0,0},{1,5},{2,2},{3,7},{4,4},{5,1},{6,6},{7,3},{8,8},{9,13},{10,1... | collective-permute-start | bytes 196616 | tf_op jit(solution)/shard_map/ppermute | solution.py:150
  9.0 6.1 %collective-permute-start.9 = (bf16[64,512]{1,0:T(8,128)(2,1)S(1)}, bf16[64,512]{1,0:T(8,128)(2,1)S(1)}, u32[]{:S(2)}, u32[]{:S(2)}) collective-permute-start(bf16[64,512]{1,0:T(8,128)(2,1)S(1)} %collective-permute-done.5.block), channel_id=1, source_target_pairs={{0,2},{1,3},{2,0},{3,1},{4,6},{5,7},{6,4},{7,5},{8,10},{9,11},{10,... | collective-permute-start | bytes 196616 | tf_op jit(solution)/shard_map/ppermute | solution.py:150
  10.6 4.8 %collective-permute-start.8 = (bf16[64,512]{1,0:T(8,128)(2,1)S(1)}, bf16[64,512]{1,0:T(8,128)(2,1)S(1)}, u32[]{:S(2)}, u32[]{:S(2)}) collective-permute-start(bf16[64,512]{1,0:T(8,128)(2,1)S(1)} %collective-permute-done.7), channel_id=1, source_target_pairs={{0,2},{1,3},{2,0},{3,1},{4,6},{5,7},{6,4},{7,5},{8,10},{9,11},{10,... | collective-permute-start | bytes 196616 | tf_op jit(solution)/shard_map/ppermute | solution.py:150
  11.1 1.4 %collective-permute-start = (bf16[64,512]{1,0:T(8,128)(2,1)S(1)}, bf16[64,512]{1,0:T(8,128)(2,1)S(1)}, u32[]{:S(2)}, u32[]{:S(2)}) collective-permute-start(bf16[64,512]{1,0:T(8,128)(2,1)S(1)} %get-tuple-element.24.rows), channel_id=1, source_target_pairs={{0,1},{1,0},{2,3},{3,2},{4,5},{5,4},{6,7},{7,6},{8,9},{9,8},{10,11... | collective-permute-start | bytes 196616 | tf_op jit(solution)/shard_map/cond/branch_1_fun/ppermute | solution.py:150
  12.2 1.4 %collective-permute-start.1 = (bf16[64,1024]{1,0:T(8,128)(2,1)S(1)}, bf16[64,1024]{1,0:T(8,128)(2,1)S(1)}, u32[]{:S(2)}, u32[]{:S(2)}) collective-permute-start(bf16[64,1024]{1,0:T(8,128)(2,1)S(1)} %branch_1_fun.7), channel_id=1, source_target_pairs={{0,1},{1,0},{2,3},{3,2},{4,5},{5,4},{6,7},{7,6},{8,9},{9,8},{10,11... | collective-permute-start | bytes 393224 | tf_op jit(solution)/shard_map/cond/branch_1_fun/ppermute | solution.py:150
  13.6 11.2 %collective-permute-start.6 = (bf16[64,1024]{1,0:T(8,128)(2,1)S(1)}, bf16[64,1024]{1,0:T(8,128)(2,1)S(1)}, u32[]{:S(2)}, u32[]{:S(2)}) collective-permute-start(bf16[64,1024]{1,0:T(8,128)(2,1)S(1)} %get-tuple-element.64), channel_id=1, source_target_pairs={{0,8},{1,13},{2,10},{3,15},{4,12},{5,9},{6,14},{7,11},{8,0},{9,5},... | collective-permute-start | bytes 393224 | tf_op jit(solution)/shard_map/ppermute | solution.py:150
  15.4 2.8 %collective-permute-start.2 = (bf16[192,512]{1,0:T(8,128)(2,1)S(1)}, bf16[192,512]{1,0:T(8,128)(2,1)S(1)}, u32[]{:S(2)}, u32[]{:S(2)}) collective-permute-start(bf16[192,512]{1,0:T(8,128)(2,1)S(1)} %get-tuple-element.28.rows), channel_id=1, source_target_pairs={{0,1},{1,0},{2,3},{3,2},{4,5},{5,4},{6,7},{7,6},{8,9},{9,8},{10,11... | collective-permute-start | bytes 589832 | tf_op jit(solution)/shard_map/cond/branch_1_fun/ppermute | solution.py:150
  17.8 1.8 %collective-permute-start.3 = (bf16[192,1024]{1,0:T(8,128)(2,1)S(1)}, bf16[192,1024]{1,0:T(8,128)(2,1)S(1)}, u32[]{:S(2)}, u32[]{:S(2)}) collective-permute-start(bf16[192,1024]{1,0:T(8,128)(2,1)S(1)} %branch_1_fun.10), channel_id=1, source_target_pairs={{0,1},{1,0},{2,3},{3,2},{4,5},{5,4},{6,7},{7,6},{8,9},{9,8},{10,11... | collective-permute-start | bytes 1179656 | tf_op jit(solution)/shard_map/cond/branch_1_fun/ppermute | solution.py:150
  19.7 9.8 %collective-permute-start.10 = (bf16[64,1024]{1,0:T(8,128)(2,1)S(1)}, bf16[64,1024]{1,0:T(8,128)(2,1)S(1)}, u32[]{:S(2)}, u32[]{:S(2)}) collective-permute-start(bf16[64,1024]{1,0:T(8,128)(2,1)S(1)} %get-tuple-element.50), channel_id=1, source_target_pairs={{0,10},{1,15},{2,8},{3,13},{4,14},{5,11},{6,12},{7,9},{8,2},{9,7},... | collective-permute-start | bytes 393224 | tf_op jit(solution)/shard_map/ppermute | solution.py:150
  20.4 9.3 %collective-permute-start.11 = (bf16[64,1024]{1,0:T(8,128)(2,1)S(1)}, bf16[64,1024]{1,0:T(8,128)(2,1)S(1)}, u32[]{:S(2)}, u32[]{:S(2)}) collective-permute-start(bf16[64,1024]{1,0:T(8,128)(2,1)S(1)} %get-tuple-element.51), channel_id=1, source_target_pairs={{0,4},{1,1},{2,6},{3,3},{4,0},{5,5},{6,2},{7,7},{8,12},{9,9},{10,1... | collective-permute-start | bytes 393224 | tf_op jit(solution)/shard_map/ppermute | solution.py:150
  24.3 6.3 %collective-permute-start.12 = (bf16[32,1024]{1,0:T(8,128)(2,1)S(1)}, bf16[32,1024]{1,0:T(8,128)(2,1)S(1)}, u32[]{:S(2)}, u32[]{:S(2)}) collective-permute-start(bf16[32,1024]{1,0:T(8,128)(2,1)S(1)} %get-tuple-element.52), channel_id=1, source_target_pairs={{0,6},{1,3},{2,4},{3,1},{4,2},{5,7},{6,0},{7,5},{8,14},{9,11},{10,... | collective-permute-start | bytes 196616 | tf_op jit(solution)/shard_map/ppermute | solution.py:150
  24.8 6.5 %collective-permute-start.13 = (bf16[32,1024]{1,0:T(8,128)(2,1)S(1)}, bf16[32,1024]{1,0:T(8,128)(2,1)S(1)}, u32[]{:S(2)}, u32[]{:S(2)}) collective-permute-start(bf16[32,1024]{1,0:T(8,128)(2,1)S(1)} %get-tuple-element.53), channel_id=1, source_target_pairs={{0,7},{1,2},{2,5},{3,0},{4,3},{5,6},{6,1},{7,4},{8,15},{9,10},{10,... | collective-permute-start | bytes 196616 | tf_op jit(solution)/shard_map/ppermute | solution.py:150
  29.7 1.6 %collective-permute-start.14 = (f32[32,1024]{1,0:T(8,128)S(1)}, f32[32,1024]{1,0:T(8,128)S(1)}, u32[]{:S(2)}, u32[]{:S(2)}) collective-permute-start(f32[32,1024]{1,0:T(8,128)S(1)} %get-tuple-element.54), channel_id=1, source_target_pairs={{0,1},{1,0},{2,3},{3,2},{4,5},{5,4},{6,7},{7,6},{8,9},{9,8},{10,11... | collective-permute-start | bytes 393224 | tf_op jit(solution)/shard_map/ppermute | solution.py:150

commit v6 on v5

--- a/solution.py
+++ b/solution.py
@@ -176,26 +176,29 @@
             return [jnp.zeros((size, whitening.shape[1]), jnp.bfloat16) for size in sizes]
 
         go = lax.axis_index("lm") >= 0
-        groups = [[(i, k) for i in range(outer // 2)] for k in range(inner)]
-        groups[1].insert(0, groups[0].pop(0))
-        parts, last = [], []
+        groups = [[(i, k) for i in range(1, outer // 2)] for k in range(inner)]
+        groups.append([(0, k) for k in range(inner)])
+        total, last = None, []
         for group in groups:
             first = [lines[k][i] for i, k in group]
+            if group == groups[-1]:
+                first[0], held[0] = lax.optimization_barrier((first[0], held[0]))
             first = jnp.concatenate(first) if len(first) > 1 else copy(*first)
             sizes = []
             for where in group:
-                sizes += [rows, rows] if where == (0, inner - 1) else [2 * rows]
+                sizes += [rows, rows] if where[0] == 0 else [2 * rows]
             work, none = (functools.partial(branch, sizes) for branch in (line_sums, nothing))
             blocks = lax.cond(go, work, none, first, landmarks, land_sq, whitening)
+            held = list(blocks)
+            parts = [] if total is None else [total]
             for i, k in reversed(group):
                 by = (steps[1][i] * inner + k, steps[0][i] * inner + k)
                 block = blocks.pop()
-                if (i, k) == (0, inner - 1):
-                    last = [exchange(block, by), exchange(blocks.pop(), by, 1)]
+                if i == 0:
+                    last += [exchange(block, by), exchange(blocks.pop(), by, 1)]
                 else:
                     parts.append(exchange(block, by))
-        early = outer // 2 - 1
-        total = add(add(*parts[:early]), *parts[early:])
+            total = add(*parts) if len(parts) > (total is not None) else total
         return add(total[rows:], *last) + swap(total[:rows])
 
     return jax.shard_map(

time: 32.2 us -> 32 us (level)
  waiting for transfers between devices: 9.13 us -> 6.07 us
  starting transfers between devices: 17.2 us -> 18.9 us
  Pallas kernels: 4.06 us -> 5.04 us
    ppermute x15 -> x18, waiting for transfers between devices: 9.13 us -> 6.07 us  [exchange(): return lax.ppermute(block, AXES, pairs)]
    ppermute x15 -> x18, starting transfers between devices: 17.2 us -> 18.9 us  [exchange(): return lax.ppermute(block, AXES, pairs)]
    pallas_call x4 -> x6, Pallas kernels: 2.4 us -> 3.36 us  [line_part(): pl.pallas_call(sums_body, out_shape=jax.ShapeDtypeStruct((count, width),...]
  transfers between devices with their start and end apart: 15 -> 18, of which waited for: 11 -> 12; matrix products, arithmetic and copies ran while one was open for 2% -> 2% of each run, Pallas kernels for 13% -> 16%
where the time goes in v6:
time: 32 us; the launch traced here: 31.7 us
  starting transfers between devices  18.9 us (59%)
  waiting for transfers between devices  6.07 us (19%)
  Pallas kernels  5.04 us (16%)
  local copies, waits for them, and re-layouts  0.78 us (2%)
  other arithmetic  0.68 us (2%)
    ppermute x18, starting transfers between devices, exchange(): return lax.ppermute(block, AXES, pairs)  18.9 us
    ppermute x18, waiting for transfers between devices, exchange(): return lax.ppermute(block, AXES, pairs)  6.07 us
    pallas_call x6, Pallas kernels, line_part(): pl.pallas_call(sums_body, out_shape=jax.ShapeDtypeStruct((count, width),...  3.36 us
    pallas_call x1, Pallas kernels, load(): pl.pallas_call(load_body, out_shape=[jax.ShapeDtypeStruct(landmarks.shape...  1.49 us
    unnamed x1, local copies, waits for them, and re-layouts  0.76 us
    add x1, other arithmetic, local(): return add(total[rows:], *last) + swap(total[:rows])  0.67 us
  transfers between devices with their start and end apart: 18, of which 12 were waited for; matrix products, arithmetic and copies ran while one was open for 2% of the time, Pallas kernels for 16%

profile of v6, /device:TPU:0, one launch (start us, length us, event | category | flops | bytes accessed | tf_op | source)
XLA Modules:
  0.0 31.7 jit_solution(3364038088998216409)
XLA Ops:
  0.5 0.8 %constant_dynamic-update-slice_fusion.1 = bf16[64,512]{1,0:T(8,128)(2,1)S(1)} fusion(bf16[32,512]{1,0:T(8,128)(2,1)} %param.9), kind=kLoop, calls=%fused_computation.2 | loop fusion | bytes 65536
  1.5 4.9 %collective-permute-start.7 = (bf16[64,512]{1,0:T(8,128)(2,1)S(1)}, bf16[64,512]{1,0:T(8,128)(2,1)S(1)}, u32[]{:S(2)}, u32[]{:S(2)}) collective-permute-start(bf16[64,512]{1,0:T(8,128)(2,1)S(1)} %constant_dynamic-update-slice_fusion), channel_id=1, source_target_pairs={{0,12},{1,9},{2,14},{3,11},{4,8},{5,13},{6,10},{7,15},{8,4},{9,1},... | collective-permute-start | bytes 196616 | tf_op jit(solution)/shard_map/ppermute | solution.py:150
  6.5 0.7 %collective-permute-start.11 = (bf16[64,512]{1,0:T(8,128)(2,1)S(1)}, bf16[64,512]{1,0:T(8,128)(2,1)S(1)}, u32[]{:S(2)}, u32[]{:S(2)}) collective-permute-start(bf16[64,512]{1,0:T(8,128)(2,1)S(1)} %constant_dynamic-update-slice_fusion), channel_id=1, source_target_pairs={{0,0},{1,5},{2,2},{3,7},{4,4},{5,1},{6,6},{7,3},{8,8},{9,13},{10,1... | collective-permute-start | bytes 196616 | tf_op jit(solution)/shard_map/ppermute | solution.py:150
  7.1 1.5 %shard_map.37 = (bf16[512,512]{1,0:T(8,128)(2,1)S(1)}, bf16[512,1024]{1,0:T(8,128)(2,1)S(1)}, f32[8,512]{1,0:T(8,128)S(1)}) custom-call(bf16[512,512]{1,0:T(8,128)(2,1)} %landmarks, bf16[512,1024]{1,0:T(8,128)(2,1)} %weights.1), custom_call_target="tpu_custom_call" | custom-call | flops 1000000000 | tf_op jit(solution)/shard_map/pallas_call | solution.py:34
  9.0 1.5 %collective-permute-start.9 = (bf16[64,512]{1,0:T(8,128)(2,1)S(1)}, bf16[64,512]{1,0:T(8,128)(2,1)S(1)}, u32[]{:S(2)}, u32[]{:S(2)}) collective-permute-start(bf16[64,512]{1,0:T(8,128)(2,1)S(1)} %collective-permute-done.7.block), channel_id=1, source_target_pairs={{0,2},{1,3},{2,0},{3,1},{4,6},{5,7},{6,4},{7,5},{8,10},{9,11},{10,... | collective-permute-start | bytes 196616 | tf_op jit(solution)/shard_map/ppermute | solution.py:150
  11.1 2.5 %conditional.3 = (bf16[64,1024]{1,0:T(8,128)(2,1)S(1)}) conditional(s32[]{:T(128)} %convert_element_type.2, () %tuple.27, (bf16[64,512]{1,0:T(8,128)(2,1)S(1)}, bf16[512,512]{1,0:T(8,128)(2,1)S(1)}, f32[8,512]{1,0:T(8,128)S(1)}, bf16[512,1024]{1,0:T(8,128)(2,1)S(1)}) %tuple.30), branch_computations={%region_0.0_spmd, %region_1.0_spmd} | conditional | flops 1107361792 | bytes 4620376 | solution.py:191
  12.5 0.5 %branch_1_fun.9.kept = f32[64,1024]{1,0:T(8,128)S(1)} custom-call(bf16[64,512]{1,0:T(8,128)(2,1)S(1)} %collective-permute-done.rows, bf16[512,512]{1,0:T(8,128)(2,1)S(1)} %get-tuple-element.36.landmarks, f32[8,512]{1,0:T(8,128)S(1)} %get-tuple-element.37.land_sq, bf16[512,1024]{1,0:T(8,128)(2,1)S(1)} %get-tuple-element.38.weights), custom_call_target="tpu_custom_call" | custom-call | flops 1006632960 | bytes 1654784 | tf_op jit(solution)/shard_map/cond/branch_1_fun/pallas_call | solution.py:67
  13.6 1.6 %collective-permute-start.8 = (bf16[64,1024]{1,0:T(8,128)(2,1)S(1)}, bf16[64,1024]{1,0:T(8,128)(2,1)S(1)}, u32[]{:S(2)}, u32[]{:S(2)}) collective-permute-start(bf16[64,1024]{1,0:T(8,128)(2,1)S(1)} %get-tuple-element.81), channel_id=1, source_target_pairs={{0,8},{1,13},{2,10},{3,15},{4,12},{5,9},{6,14},{7,11},{8,0},{9,5},... | collective-permute-start | bytes 393224 | tf_op jit(solution)/shard_map/ppermute | solution.py:150
  15.2 4.0 %conditional.4 = (bf16[64,1024]{1,0:T(8,128)(2,1)S(1)}) conditional(s32[]{:T(128)} %convert_element_type.2, () %tuple.31, (bf16[64,512]{1,0:T(8,128)(2,1)S(1)}, bf16[512,512]{1,0:T(8,128)(2,1)S(1)}, f32[8,512]{1,0:T(8,128)S(1)}, bf16[512,1024]{1,0:T(8,128)(2,1)S(1)}) %tuple.32), branch_computations={%region_2.0_spmd, %region_3.0_spmd} | conditional | flops 1107361792 | bytes 4620376 | solution.py:191
  15.2 2.0 %collective-permute-start.2 = (bf16[64,512]{1,0:T(8,128)(2,1)S(1)}, bf16[64,512]{1,0:T(8,128)(2,1)S(1)}, u32[]{:S(2)}, u32[]{:S(2)}) collective-permute-start(bf16[64,512]{1,0:T(8,128)(2,1)S(1)} %get-tuple-element.39.rows), channel_id=1, source_target_pairs={{0,1},{1,0},{2,3},{3,2},{4,5},{5,4},{6,7},{7,6},{8,9},{9,8},{10,11... | collective-permute-start | bytes 196616 | tf_op jit(solution)/shard_map/cond/branch_1_fun/ppermute | solution.py:150
  17.2 0.6 %branch_1_fun.13 = bf16[64,1024]{1,0:T(8,128)(2,1)S(1)} custom-call(bf16[64,512]{1,0:T(8,128)(2,1)S(1)} %get-tuple-element.39.rows, bf16[512,512]{1,0:T(8,128)(2,1)S(1)} %get-tuple-element.40.landmarks, f32[8,512]{1,0:T(8,128)S(1)} %get-tuple-element.41.land_sq, bf16[512,1024]{1,0:T(8,128)(2,1)S(1)} %get-tuple-element.42.weights), custom_call_target="tpu_custom_call" | custom-call | flops 100663296 | bytes 1654784 | tf_op jit(solution)/shard_map/cond/branch_1_fun/pallas_call | solution.py:67
  18.1 0.5 %branch_1_fun.12.kept = f32[64,1024]{1,0:T(8,128)S(1)} custom-call(bf16[64,512]{1,0:T(8,128)(2,1)S(1)} %collective-permute-done.2.rows, bf16[512,512]{1,0:T(8,128)(2,1)S(1)} %get-tuple-element.40.landmarks, f32[8,512]{1,0:T(8,128)S(1)} %get-tuple-element.41.land_sq, bf16[512,1024]{1,0:T(8,128)(2,1)S(1)} %get-tuple-element.42.weights), custom_call_target="tpu_custom_call" | custom-call | flops 1006632960 | bytes 1654784 | tf_op jit(solution)/shard_map/cond/branch_1_fun/pallas_call | solution.py:67
  19.2 0.7 %collective-permute-start.10 = (bf16[64,1024]{1,0:T(8,128)(2,1)S(1)}, bf16[64,1024]{1,0:T(8,128)(2,1)S(1)}, u32[]{:S(2)}, u32[]{:S(2)}) collective-permute-start(bf16[64,1024]{1,0:T(8,128)(2,1)S(1)} %get-tuple-element.82), channel_id=1, source_target_pairs={{0,10},{1,15},{2,8},{3,13},{4,14},{5,11},{6,12},{7,9},{8,2},{9,7},... | collective-permute-start | bytes 393224 | tf_op jit(solution)/shard_map/ppermute | solution.py:150
  19.9 3.1 %conditional.5 = ((bf16[32,1024]{1,0:T(8,128)(2,1)S(1)}, bf16[32,1024]{1,0:T(8,128)(2,1)S(1)}, bf16[32,1024]{1,0:T(8,128)(2,1)S(1)}, bf16[32,1024]{1,0:T(8,128)(2,1)S(1)})) conditional(s32[]{:T(128)} %convert_element_type.2, () %tuple.33, (bf16[128,512]{1,0:T(8,128)(2,1)S(1)}, bf16[512,512]{1,0:T(8,128)(2,1)S(1)}, f32[8,512]{1,0:T(8,128)S(1)}, ...), branch_computations={%region_4.0_spmd, %region_5.0_spmd} | conditional | flops 2214723584 | bytes 6062168 | solution.py:191
  19.9 0.8 %collective-permute-start.4 = (bf16[128,512]{1,0:T(8,128)(2,1)S(1)}, bf16[128,512]{1,0:T(8,128)(2,1)S(1)}, u32[]{:S(2)}, u32[]{:S(2)}) collective-permute-start(bf16[128,512]{1,0:T(8,128)(2,1)S(1)} %get-tuple-element.43.rows), channel_id=1, source_target_pairs={{0,1},{1,0},{2,3},{3,2},{4,5},{5,4},{6,7},{7,6},{8,9},{9,8},{10,11... | collective-permute-start | bytes 393224 | tf_op jit(solution)/shard_map/cond/branch_1_fun/ppermute | solution.py:150
  20.7 0.6 %branch_1_fun.16 = bf16[128,1024]{1,0:T(8,128)(2,1)S(1)} custom-call(bf16[128,512]{1,0:T(8,128)(2,1)S(1)} %get-tuple-element.43.rows, bf16[512,512]{1,0:T(8,128)(2,1)S(1)} %get-tuple-element.44.landmarks, f32[8,512]{1,0:T(8,128)S(1)} %get-tuple-element.45.land_sq, bf16[512,1024]{1,0:T(8,128)(2,1)S(1)} %get-tuple-element.46.weights), custom_call_target="tpu_custom_call" | custom-call | flops 201326592 | bytes 1720320 | tf_op jit(solution)/shard_map/cond/branch_1_fun/pallas_call | solution.py:67
  21.7 0.6 %branch_1_fun.15.kept = f32[128,1024]{1,0:T(8,128)S(1)} custom-call(bf16[128,512]{1,0:T(8,128)(2,1)S(1)} %collective-permute-done.4.rows, bf16[512,512]{1,0:T(8,128)(2,1)S(1)} %get-tuple-element.44.landmarks, f32[8,512]{1,0:T(8,128)S(1)} %get-tuple-element.45.land_sq, bf16[512,1024]{1,0:T(8,128)(2,1)S(1)} %get-tuple-element.46.weights), custom_call_target="tpu_custom_call" | custom-call | flops 2013265920 | bytes 1720320 | tf_op jit(solution)/shard_map/cond/branch_1_fun/pallas_call | solution.py:67
  22.3 0.6 %collective-permute-done.5.taken = bf16[128,1024]{1,0:T(8,128)(2,1)S(1)} collective-permute-done((bf16[128,1024]{1,0:T(8,128)(2,1)S(1)}, bf16[128,1024]{1,0:T(8,128)(2,1)S(1)}, u32[]{:S(2)}, u32[]{:S(2)}) %collective-permute-start.5) | collective-permute-done | bytes 262176 | tf_op jit(solution)/shard_map/cond/branch_1_fun/ppermute | solution.py:150
  23.0 0.9 %collective-permute-start.13 = (bf16[32,1024]{1,0:T(8,128)(2,1)S(1)}, bf16[32,1024]{1,0:T(8,128)(2,1)S(1)}, u32[]{:S(2)}, u32[]{:S(2)}) collective-permute-start(bf16[32,1024]{1,0:T(8,128)(2,1)S(1)} %get-tuple-element.67), channel_id=1, source_target_pairs={{0,6},{1,3},{2,4},{3,1},{4,2},{5,7},{6,0},{7,5},{8,14},{9,11},{10,... | collective-permute-start | bytes 196616 | tf_op jit(solution)/shard_map/ppermute | solution.py:150
  23.9 0.9 %collective-permute-start.14 = (bf16[32,1024]{1,0:T(8,128)(2,1)S(1)}, bf16[32,1024]{1,0:T(8,128)(2,1)S(1)}, u32[]{:S(2)}, u32[]{:S(2)}) collective-permute-start(bf16[32,1024]{1,0:T(8,128)(2,1)S(1)} %get-tuple-element.68), channel_id=1, source_target_pairs={{0,7},{1,2},{2,5},{3,0},{4,3},{5,6},{6,1},{7,4},{8,15},{9,10},{10,... | collective-permute-start | bytes 196616 | tf_op jit(solution)/shard_map/ppermute | solution.py:150
  24.8 3.1 %collective-permute-start.15 = (bf16[32,1024]{1,0:T(8,128)(2,1)S(1)}, bf16[32,1024]{1,0:T(8,128)(2,1)S(1)}, u32[]{:S(2)}, u32[]{:S(2)}) collective-permute-start(bf16[32,1024]{1,0:T(8,128)(2,1)S(1)} %get-tuple-element.69), channel_id=1, source_target_pairs={{0,4},{1,1},{2,6},{3,3},{4,0},{5,5},{6,2},{7,7},{8,12},{9,9},{10,1... | collective-permute-start | bytes 196616 | tf_op jit(solution)/shard_map/ppermute | solution.py:150
  28.0 1.1 %collective-permute-done.10.refs_1_ = bf16[64,1024]{1,0:T(8,128)(2,1)S(1)} collective-permute-done((bf16[64,1024]{1,0:T(8,128)(2,1)S(1)}, bf16[64,1024]{1,0:T(8,128)(2,1)S(1)}, u32[]{:S(2)}, u32[]{:S(2)}) %collective-permute-start.10) | collective-permute-done | bytes 131104 | tf_op jit(solution)/shard_map/ppermute | solution.py:150
  29.7 1.1 %collective-permute-done.14.refs_2_ = bf16[32,1024]{1,0:T(8,128)(2,1)S(1)} collective-permute-done((bf16[32,1024]{1,0:T(8,128)(2,1)S(1)}, bf16[32,1024]{1,0:T(8,128)(2,1)S(1)}, u32[]{:S(2)}, u32[]{:S(2)}) %collective-permute-start.14) | collective-permute-done | bytes 65568 | tf_op jit(solution)/shard_map/ppermute | solution.py:150
  31.0 0.7 %add.3 = f32[32,1024]{1,0:T(8,128)} add(f32[32,1024]{1,0:T(8,128)S(1)} %shard_map.42, f32[32,1024]{1,0:T(8,128)S(1)} %collective-permute-done.17) | non-fusion elementwise | flops 32768 | bytes 393216 | tf_op jit(solution)/shard_map/add | solution.py:202
  (35 shorter events, 5.8 us)
Async XLA Ops:
  0.0 1.5 %collective-permute-start.6 = (bf16[32,512]{1,0:T(8,128)(2,1)}, bf16[32,512]{1,0:T(8,128)(2,1)S(1)}, u32[]{:S(2)}, u32[]{:S(2)}) collective-permute-start(bf16[32,512]{1,0:T(8,128)(2,1)} %param.9), channel_id=1, source_target_pairs={{0,1},{1,0},{2,3},{3,2},{4,5},{5,4},{6,7},{7,6},{8,9},{9,8},{10,11... | collective-permute-start | bytes 98312 | tf_op jit(solution)/shard_map/ppermute | solution.py:150
  1.5 7.5 %collective-permute-start.7 = (bf16[64,512]{1,0:T(8,128)(2,1)S(1)}, bf16[64,512]{1,0:T(8,128)(2,1)S(1)}, u32[]{:S(2)}, u32[]{:S(2)}) collective-permute-start(bf16[64,512]{1,0:T(8,128)(2,1)S(1)} %constant_dynamic-update-slice_fusion), channel_id=1, source_target_pairs={{0,12},{1,9},{2,14},{3,11},{4,8},{5,13},{6,10},{7,15},{8,4},{9,1},... | collective-permute-start | bytes 196616 | tf_op jit(solution)/shard_map/ppermute | solution.py:150
  6.5 4.1 %collective-permute-start.11 = (bf16[64,512]{1,0:T(8,128)(2,1)S(1)}, bf16[64,512]{1,0:T(8,128)(2,1)S(1)}, u32[]{:S(2)}, u32[]{:S(2)}) collective-permute-start(bf16[64,512]{1,0:T(8,128)(2,1)S(1)} %constant_dynamic-update-slice_fusion), channel_id=1, source_target_pairs={{0,0},{1,5},{2,2},{3,7},{4,4},{5,1},{6,6},{7,3},{8,8},{9,13},{10,1... | collective-permute-start | bytes 196616 | tf_op jit(solution)/shard_map/ppermute | solution.py:150
  9.0 6.1 %collective-permute-start.9 = (bf16[64,512]{1,0:T(8,128)(2,1)S(1)}, bf16[64,512]{1,0:T(8,128)(2,1)S(1)}, u32[]{:S(2)}, u32[]{:S(2)}) collective-permute-start(bf16[64,512]{1,0:T(8,128)(2,1)S(1)} %collective-permute-done.7.block), channel_id=1, source_target_pairs={{0,2},{1,3},{2,0},{3,1},{4,6},{5,7},{6,4},{7,5},{8,10},{9,11},{10,... | collective-permute-start | bytes 196616 | tf_op jit(solution)/shard_map/ppermute | solution.py:150
  10.6 9.3 %collective-permute-start.12 = (bf16[64,512]{1,0:T(8,128)(2,1)S(1)}, bf16[64,512]{1,0:T(8,128)(2,1)S(1)}, u32[]{:S(2)}, u32[]{:S(2)}) collective-permute-start(bf16[64,512]{1,0:T(8,128)(2,1)S(1)} %collective-permute-done.11), channel_id=1, source_target_pairs={{0,2},{1,3},{2,0},{3,1},{4,6},{5,7},{6,4},{7,5},{8,10},{9,11},{10,... | collective-permute-start | bytes 196616 | tf_op jit(solution)/shard_map/ppermute | solution.py:150
  11.1 1.4 %collective-permute-start = (bf16[64,512]{1,0:T(8,128)(2,1)S(1)}, bf16[64,512]{1,0:T(8,128)(2,1)S(1)}, u32[]{:S(2)}, u32[]{:S(2)}) collective-permute-start(bf16[64,512]{1,0:T(8,128)(2,1)S(1)} %get-tuple-element.34.rows), channel_id=1, source_target_pairs={{0,1},{1,0},{2,3},{3,2},{4,5},{5,4},{6,7},{7,6},{8,9},{9,8},{10,11... | collective-permute-start | bytes 196616 | tf_op jit(solution)/shard_map/cond/branch_1_fun/ppermute | solution.py:150
  12.2 1.4 %collective-permute-start.1 = (bf16[64,1024]{1,0:T(8,128)(2,1)S(1)}, bf16[64,1024]{1,0:T(8,128)(2,1)S(1)}, u32[]{:S(2)}, u32[]{:S(2)}) collective-permute-start(bf16[64,1024]{1,0:T(8,128)(2,1)S(1)} %branch_1_fun.10), channel_id=1, source_target_pairs={{0,1},{1,0},{2,3},{3,2},{4,5},{5,4},{6,7},{7,6},{8,9},{9,8},{10,11... | collective-permute-start | bytes 393224 | tf_op jit(solution)/shard_map/cond/branch_1_fun/ppermute | solution.py:150
  13.6 14.3 %collective-permute-start.8 = (bf16[64,1024]{1,0:T(8,128)(2,1)S(1)}, bf16[64,1024]{1,0:T(8,128)(2,1)S(1)}, u32[]{:S(2)}, u32[]{:S(2)}) collective-permute-start(bf16[64,1024]{1,0:T(8,128)(2,1)S(1)} %get-tuple-element.81), channel_id=1, source_target_pairs={{0,8},{1,13},{2,10},{3,15},{4,12},{5,9},{6,14},{7,11},{8,0},{9,5},... | collective-permute-start | bytes 393224 | tf_op jit(solution)/shard_map/ppermute | solution.py:150
  15.2 2.9 %collective-permute-start.2 = (bf16[64,512]{1,0:T(8,128)(2,1)S(1)}, bf16[64,512]{1,0:T(8,128)(2,1)S(1)}, u32[]{:S(2)}, u32[]{:S(2)}) collective-permute-start(bf16[64,512]{1,0:T(8,128)(2,1)S(1)} %get-tuple-element.39.rows), channel_id=1, source_target_pairs={{0,1},{1,0},{2,3},{3,2},{4,5},{5,4},{6,7},{7,6},{8,9},{9,8},{10,11... | collective-permute-start | bytes 196616 | tf_op jit(solution)/shard_map/cond/branch_1_fun/ppermute | solution.py:150
  17.7 1.4 %collective-permute-start.3 = (bf16[64,1024]{1,0:T(8,128)(2,1)S(1)}, bf16[64,1024]{1,0:T(8,128)(2,1)S(1)}, u32[]{:S(2)}, u32[]{:S(2)}) collective-permute-start(bf16[64,1024]{1,0:T(8,128)(2,1)S(1)} %branch_1_fun.13), channel_id=1, source_target_pairs={{0,1},{1,0},{2,3},{3,2},{4,5},{5,4},{6,7},{7,6},{8,9},{9,8},{10,11... | collective-permute-start | bytes 393224 | tf_op jit(solution)/shard_map/cond/branch_1_fun/ppermute | solution.py:150
  19.2 10.0 %collective-permute-start.10 = (bf16[64,1024]{1,0:T(8,128)(2,1)S(1)}, bf16[64,1024]{1,0:T(8,128)(2,1)S(1)}, u32[]{:S(2)}, u32[]{:S(2)}) collective-permute-start(bf16[64,1024]{1,0:T(8,128)(2,1)S(1)} %get-tuple-element.82), channel_id=1, source_target_pairs={{0,10},{1,15},{2,8},{3,13},{4,14},{5,11},{6,12},{7,9},{8,2},{9,7},... | collective-permute-start | bytes 393224 | tf_op jit(solution)/shard_map/ppermute | solution.py:150
  19.9 1.8 %collective-permute-start.4 = (bf16[128,512]{1,0:T(8,128)(2,1)S(1)}, bf16[128,512]{1,0:T(8,128)(2,1)S(1)}, u32[]{:S(2)}, u32[]{:S(2)}) collective-permute-start(bf16[128,512]{1,0:T(8,128)(2,1)S(1)} %get-tuple-element.43.rows), channel_id=1, source_target_pairs={{0,1},{1,0},{2,3},{3,2},{4,5},{5,4},{6,7},{7,6},{8,9},{9,8},{10,11... | collective-permute-start | bytes 393224 | tf_op jit(solution)/shard_map/cond/branch_1_fun/ppermute | solution.py:150
  21.3 1.6 %collective-permute-start.5 = (bf16[128,1024]{1,0:T(8,128)(2,1)S(1)}, bf16[128,1024]{1,0:T(8,128)(2,1)S(1)}, u32[]{:S(2)}, u32[]{:S(2)}) collective-permute-start(bf16[128,1024]{1,0:T(8,128)(2,1)S(1)} %branch_1_fun.16), channel_id=1, source_target_pairs={{0,1},{1,0},{2,3},{3,2},{4,5},{5,4},{6,7},{7,6},{8,9},{9,8},{10,11... | collective-permute-start | bytes 786440 | tf_op jit(solution)/shard_map/cond/branch_1_fun/ppermute | solution.py:150
  23.0 6.7 %collective-permute-start.13 = (bf16[32,1024]{1,0:T(8,128)(2,1)S(1)}, bf16[32,1024]{1,0:T(8,128)(2,1)S(1)}, u32[]{:S(2)}, u32[]{:S(2)}) collective-permute-start(bf16[32,1024]{1,0:T(8,128)(2,1)S(1)} %get-tuple-element.67), channel_id=1, source_target_pairs={{0,6},{1,3},{2,4},{3,1},{4,2},{5,7},{6,0},{7,5},{8,14},{9,11},{10,... | collective-permute-start | bytes 196616 | tf_op jit(solution)/shard_map/ppermute | solution.py:150
  23.9 6.9 %collective-permute-start.14 = (bf16[32,1024]{1,0:T(8,128)(2,1)S(1)}, bf16[32,1024]{1,0:T(8,128)(2,1)S(1)}, u32[]{:S(2)}, u32[]{:S(2)}) collective-permute-start(bf16[32,1024]{1,0:T(8,128)(2,1)S(1)} %get-tuple-element.68), channel_id=1, source_target_pairs={{0,7},{1,2},{2,5},{3,0},{4,3},{5,6},{6,1},{7,4},{8,15},{9,10},{10,... | collective-permute-start | bytes 196616 | tf_op jit(solution)/shard_map/ppermute | solution.py:150
  24.8 6.1 %collective-permute-start.15 = (bf16[32,1024]{1,0:T(8,128)(2,1)S(1)}, bf16[32,1024]{1,0:T(8,128)(2,1)S(1)}, u32[]{:S(2)}, u32[]{:S(2)}) collective-permute-start(bf16[32,1024]{1,0:T(8,128)(2,1)S(1)} %get-tuple-element.69), channel_id=1, source_target_pairs={{0,4},{1,1},{2,6},{3,3},{4,0},{5,5},{6,2},{7,7},{8,12},{9,9},{10,1... | collective-permute-start | bytes 196616 | tf_op jit(solution)/shard_map/ppermute | solution.py:150
  27.9 3.1 %collective-permute-start.16 = (bf16[32,1024]{1,0:T(8,128)(2,1)S(1)}, bf16[32,1024]{1,0:T(8,128)(2,1)S(1)}, u32[]{:S(2)}, u32[]{:S(2)}) collective-permute-start(bf16[32,1024]{1,0:T(8,128)(2,1)S(1)} %get-tuple-element.70), channel_id=1, source_target_pairs={{0,5},{1,0},{2,7},{3,2},{4,1},{5,4},{6,3},{7,6},{8,13},{9,8},{10,1... | collective-permute-start | bytes 196616 | tf_op jit(solution)/shard_map/ppermute | solution.py:150
  29.2 1.8 %collective-permute-start.17 = (f32[32,1024]{1,0:T(8,128)S(1)}, f32[32,1024]{1,0:T(8,128)S(1)}, u32[]{:S(2)}, u32[]{:S(2)}) collective-permute-start(f32[32,1024]{1,0:T(8,128)S(1)} %get-tuple-element.71), channel_id=1, source_target_pairs={{0,1},{1,0},{2,3},{3,2},{4,5},{5,4},{6,7},{7,6},{8,9},{9,8},{10,11... | collective-permute-start | bytes 393224 | tf_op jit(solution)/shard_map/ppermute | solution.py:150
